TPU v7x, 512 devices: a whole 4x8x8 slice. The times are simulated.
512 devices in a mesh: lag: 8 (over y_lo, core), space: 64 (over x, y_hi, z).
Axes of the slice: x: 4, y: 8 (y_hi: 2, y_lo: 4; y = y_hi * 4 + y_lo), z: 8, core: 2. Of those that a mesh axis runs over, the one named last changes fastest.
Arguments:
- states: bfloat16 [8, 80, 127, 8192], P('lag', None, None, 'space'), may hold values from -6 to 6
- obs_weights: bfloat16 [24, 127], replicated, may hold values from -0.5 to 0.5
- observations: float32 [24, 8192], P(None, 'space'), may hold values from -6 to 6
- obs_precision: float32 [24, 8192], P(None, 'space'), may hold values from 0.3 to 3
- resample_index: int32 [1024, 80], P('space'), may hold values from 0 to 79
- blend_weight: float32 [1024], P('space'), may hold values from 0.2 to 0.7
- stencil_region: int32 [8192], P('space'), may hold values from 0 to 1023, as said below
- stencil_weight: float32 [8192], P('space'), may hold values from 0.5 to 1
Outputs:
- analysis: bfloat16 [8, 80, 127, 8192], P('lag', None, None, 'space')
Inputs may be any that keep to these rules, and one draw needn't show every extreme that they name: `resample_index`: each entry names one of the 80 members. `stencil_region`: column c lies in region c // 8; its entry is that region or the region before or after it; the first column of a region names the region before it and the last column the region after it, wherever those exist.
All inputs are finite; a program needn't handle non-finite values.
Results may differ from a plain program's by a relative error of at most 0.0012.
The roundings to bfloat16 on the way count: a program that leaves them out, or rounds other values in their place, can miss the bound.
Values may be sent and summed in bfloat16 or wider, within the bound.
A program may use at most 64 MiB of HBM per device.

v0:
```python
import math

import jax
import jax.numpy as jnp
from jax import lax
from jax.experimental import pallas as pl
from jax.experimental.pallas import tpu as pltpu
from jax.sharding import PartitionSpec as P

M = 80
LEV = 127
NOBS = 24
COLS = 128
WIDTH = 8
REG = 16
NS_ITERS = 8
KB = 256
MX = 96
GROUP = 8
F32 = jnp.float32
BF16 = jnp.bfloat16
MESH = pl.DeviceIdType.MESH

TAPER = [
    [math.exp(-0.5 * ((q * WIDTH + k - (3 * WIDTH - 1) / 2.0) / WIDTH) ** 2) for k in range(WIDTH)]
    for q in range(3)
]
PIECES = ((0, 8), (8, 8), (16, 2))


def split(x):
    high = x.astype(BF16)
    return high, (x - high.astype(F32)).astype(BF16)


def halves(x):
    high, low = split(x)
    return jnp.concatenate([high, low], axis=1)


def product(a, b):
    gap = jnp.zeros((128 - M, 256), BF16)
    out = jnp.dot(a, jnp.concatenate([b, gap, b, gap], axis=0), preferred_element_type=F32)
    return out[:, :128] + out[:, 128:]


def pair_rows(value, spread, chosen):
    first = value.astype(BF16)
    rest = value - first.astype(F32)
    second = rest.astype(BF16)
    third = (rest - second.astype(F32)).astype(BF16)
    dims = (((0,), (0,)), ((), ()))
    total = lax.dot_general(first, spread, dims, preferred_element_type=F32)
    total += lax.dot_general(second, spread, dims, preferred_element_type=F32)
    total += lax.dot_general(third, spread, dims, preferred_element_type=F32)
    return jnp.sum(jnp.where(chosen, total, 0.0).reshape(REG, WIDTH, KB), axis=1)


def prepare(w, y, pr, wb, yrow, rrow):
    row = lax.broadcasted_iota(jnp.int32, (NOBS, KB), 0)
    lane = lax.broadcasted_iota(jnp.int32, (NOBS, KB), 1)
    spread = jnp.where((lane % NOBS == row) & (lane < WIDTH * NOBS), 1.0, 0.0).astype(BF16)
    row = lax.broadcasted_iota(jnp.int32, (COLS, KB), 0)
    lane = lax.broadcasted_iota(jnp.int32, (COLS, KB), 1)
    chosen = lane // NOBS == row % WIDTH
    yrow[...] = pair_rows(y[...], spread, chosen)
    rrow[...] = pair_rows(jnp.sqrt(pr[...]), spread, chosen)
    wide = lax.dot_general(w[...], spread, (((0,), (0,)), ((), ())), preferred_element_type=F32)
    wide = jnp.concatenate([wide, jnp.zeros((1, KB), F32)], axis=0)
    for k in range(WIDTH):
        wb[k * 128 : (k + 1) * 128] = jnp.where(lane // NOBS == k, wide, 0.0).astype(BF16)


def scaled_blocks(regions, xc, wb, yrow, rrow):
    rows = []
    for r in regions:
        rows.append(jnp.concatenate([xc[r * WIDTH + k] for k in range(WIDTH)], axis=1))
    out = jnp.dot(jnp.concatenate(rows, axis=0), wb[...], preferred_element_type=F32)
    top = lax.broadcasted_iota(jnp.int32, (MX - M, KB), 0) == 0
    blocks = []
    for k, r in enumerate(regions):
        obs = out[k * M : (k + 1) * M]
        mean = jnp.sum(obs, axis=0, keepdims=True) * (1.0 / M)
        innovation = jnp.where(top, yrow[pl.ds(r, 1), :] - mean, 0.0)
        blocks.append(
            jnp.concatenate([obs - mean, innovation], axis=0) * rrow[pl.ds(r, 1), :]
        )
    return blocks


def gram_parts(x, parts):
    high, low = split(x)
    across = jnp.concatenate([x, jnp.zeros((128 - MX, KB), F32)], axis=0).T
    highs, lows = [], []
    for q in parts:
        tapered = [across[k * NOBS : (k + 1) * NOBS] * TAPER[q][k] for k in range(WIDTH)]
        h, l = split(jnp.concatenate(tapered, axis=0))
        highs.append(h)
        lows.append(l)
    used = WIDTH * NOBS
    n = 128 * len(parts)
    right = jnp.concatenate(highs + lows, axis=1)
    out = jnp.dot(high[:, :used], right, preferred_element_type=F32)
    out2 = jnp.dot(low[:, :used], right[:, :n], preferred_element_type=F32)
    total = out[:, :n] + out[:, n:] + out2
    return [total[:, k * 128 : (k + 1) * 128] for k in range(len(parts))]


def add_block(x, r, gram):
    parts = gram_parts(x, (0, 1, 2))
    gram[r + 2] += parts[0]
    gram[r + 1] += parts[1]
    gram[r] += parts[2]


def transforms_group(first, gram, resample, blend, t, ys, zs):
    row = lax.broadcasted_iota(jnp.int32, (M, 128), 0)
    col = lax.broadcasted_iota(jnp.int32, (M, 128), 1)
    eye = (row == col).astype(F32)
    norms = []
    regions = [lax.rem(first + k + 12, REG) for k in range(GROUP)]
    for k, r in enumerate(regions):
        cross = jnp.where(col < M, gram[r + 1, :M, :], 0.0)
        square = jnp.sum(cross * cross, axis=0, keepdims=True)
        norm = 1.0 + jnp.sqrt(jnp.sum(square, axis=1, keepdims=True)) * (1.0 / (M - 1))
        norms.append(norm)
        y = (eye + cross * (1.0 / (M - 1))) / norm
        e = halves(1.5 * eye - 0.5 * y)
        ys[k] = halves(product(halves(y), e))
        zs[k] = e

    @pl.loop(0, NS_ITERS - 2)
    def _(sweep):
        factors = [
            halves(1.5 * eye - 0.5 * product(zs[k], ys[k])) for k in range(GROUP)
        ]
        for k in range(GROUP):
            both = product(jnp.concatenate([ys[k], zs[k]], axis=0), factors[k])
            ys[k] = halves(both[:M])
            zs[k] = halves(both[M:])

    for k, r in enumerate(regions):
        e = halves(1.5 * eye - 0.5 * product(zs[k], ys[k]))
        root = product(zs[k], e) / jnp.sqrt(norms[k])
        drive = gram[r + 1, :M, M : M + 1]
        half = jnp.sum(root * drive, axis=0, keepdims=True)
        mean_weight = jnp.sum(root * half, axis=1, keepdims=True) * (1.0 / (M - 1))
        weights = mean_weight + root
        etkf = 1.0 / M + weights - jnp.sum(weights, axis=0, keepdims=True) * (1.0 / M)
        drawn = (resample[pl.ds(r, 1), :] == row).astype(F32)
        share = blend[r]
        t[first + k] = ((1.0 - share) * etkf + share * drawn).astype(BF16)


def make_transform_kernel(lags, spaces):
    last = lags - 1

    def kernel(
        st, w, y, pr, resample, blend, t_out, s_out,
        xc, sc, wb, yrow, rrow, edge, halo, gram, t, ys, zs,
        x_send, x_recv, e_send, e_recv, p_next, p_side, p_recv, local,
    ):
        lag = lax.axis_index("lag")
        here = lax.axis_index("space")
        odd = lax.rem(lag, 2)
        has_left, has_right = here > 0, here < spaces - 1
        left, right = here - 1, here + 1
        barrier = pltpu.get_barrier_semaphore()

        def greet(where):
            pl.semaphore_signal(barrier, inc=1, device_id=where, device_id_type=MESH)

        @pl.when(lag == last)
        def _():
            @pl.when(has_left)
            def _():
                greet({"space": left})

            @pl.when(has_right)
            def _():
                greet({"space": right})

        @pl.when(lag < last)
        def _():
            greet({"lag": lag + 1 + odd})

        def columns_first():
            for k in range(0, 128, 16):
                stop = min(k + 16, LEV)
                sc[:, k:stop, :M] = jnp.transpose(st[k:stop], (2, 0, 1))
            pltpu.make_async_copy(sc, s_out, local.at[0]).start()

        def side(p):
            first, count = PIECES[p]
            ref = t.at[pl.ds(first, count)]
            return pltpu.make_async_remote_copy(
                src_ref=ref, dst_ref=ref, send_sem=p_side.at[p], recv_sem=p_recv.at[p],
                device_id={"lag": lag - 1}, device_id_type=MESH)

        def onward(p):
            first, count = PIECES[p]
            ref = t.at[pl.ds(first, count)]
            return pltpu.make_async_remote_copy(
                src_ref=ref, dst_ref=ref, send_sem=p_next.at[p], recv_sem=p_recv.at[p],
                device_id={"lag": lag - 2}, device_id_type=MESH)

        def block_copy(k, where):
            return pltpu.make_async_remote_copy(
                src_ref=edge.at[k], dst_ref=halo.at[1 - k], send_sem=x_send.at[k],
                recv_sem=x_recv.at[1 - k], device_id={"space": where}, device_id_type=MESH)

        def edge_copy(k, where):
            return pltpu.make_async_remote_copy(
                src_ref=t.at[4 if k == 0 else 3], dst_ref=t.at[17 - k], send_sem=e_send.at[k],
                recv_sem=e_recv.at[1 - k], device_id={"space": where}, device_id_type=MESH)

        sides = ((0, has_left, left), (1, has_right, right))

        @pl.when(lag == last)
        def _():
            prepare(w, y, pr, wb, yrow, rrow)
            xc[...] = jnp.transpose(
                jnp.concatenate([st[...], jnp.zeros((1, M, COLS), BF16)], axis=0), (2, 1, 0))

            @pl.loop(0, REG + 2)
            def _(r):
                gram[r] = jnp.zeros((MX, 128), F32)

            ends = scaled_blocks((0, REG - 1), xc, wb, yrow, rrow)
            edge[0], edge[1] = ends
            pl.semaphore_wait(
                barrier, 2 + has_left.astype(jnp.int32) + has_right.astype(jnp.int32))
            for k, there, where in sides:
                @pl.when(there)
                def _(k=k, where=where):
                    block_copy(k, where).start()
            add_block(edge[0], 0, gram)
            add_block(edge[1], REG - 1, gram)

            @pl.loop(0, (REG - 2) // 2)
            def _(i):
                pair = (1 + 2 * i, 2 + 2 * i)
                for r, x in zip(pair, scaled_blocks(pair, xc, wb, yrow, rrow)):
                    add_block(x, r, gram)

            for k, there, where in sides:
                @pl.when(there)
                def _(k=k, where=where):
                    block_copy(1 - k, where).wait_recv()
                    block_copy(k, where).wait_send()

            @pl.when(has_left)
            def _():
                gram[1] += gram_parts(halo[0], (0,))[0]

            @pl.when(has_right)
            def _():
                gram[REG] += gram_parts(halo[1], (2,))[0]

            for p in range(2):
                transforms_group(p * GROUP, gram, resample, blend, t, ys, zs)
                side(p).start()
                onward(p).start()
                if p == 0:
                    for k, there, where in sides:
                        @pl.when(there)
                        def _(k=k, where=where):
                            edge_copy(k, where).start()
            for k, there, where in sides:
                @pl.when(there)
                def _(k=k, where=where):
                    edge_copy(1 - k, where).wait_recv()
                    edge_copy(k, where).wait_send()

                @pl.when(jnp.logical_not(there))
                def _(k=k):
                    t[16 + k] = jnp.zeros((M, 128), BF16)
            side(2).start()
            onward(2).start()
            columns_first()
            for p in range(3):
                side(p).wait_send()
                onward(p).wait_send()

        @pl.when(lag < last)
        def _():
            columns_first()

            @pl.when(odd == 1)
            def _():
                pl.semaphore_wait(barrier, 1 + (lag > 1).astype(jnp.int32))

            for p in range(3):
                side(p).wait_recv()

                @pl.when(odd == 1)
                def _(p=p):
                    side(p).start()

                    @pl.when(lag > 1)
                    def _():
                        onward(p).start()

            @pl.when(odd == 1)
            def _():
                for p in range(3):
                    side(p).wait_send()

                    @pl.when(lag > 1)
                    def _(p=p):
                        onward(p).wait_send()

        out = pltpu.make_async_copy(t, t_out, local.at[1])
        out.start()
        pltpu.make_async_copy(sc, s_out, local.at[0]).wait()
        out.wait()

    return kernel


def transforms_call(lags, spaces, st, w, y, pr, resample, blend):
    vmem = pl.BlockSpec(memory_space=pltpu.VMEM)
    hbm = pl.BlockSpec(memory_space=pl.ANY)
    smem = pl.BlockSpec(memory_space=pltpu.SMEM)
    dma = pltpu.SemaphoreType.DMA
    return pl.pallas_call(
        make_transform_kernel(lags, spaces),
        out_shape=(
            jax.ShapeDtypeStruct((REG + 2, M, 128), BF16),
            jax.ShapeDtypeStruct((COLS, 128, 128), BF16),
        ),
        in_specs=[vmem, vmem, vmem, vmem, vmem, smem],
        out_specs=(hbm, hbm),
        scratch_shapes=[
            pltpu.VMEM((COLS, M, 128), BF16),
            pltpu.VMEM((COLS, 128, 128), BF16),
            pltpu.VMEM((WIDTH * 128, KB), BF16),
            pltpu.VMEM((REG, KB), F32),
            pltpu.VMEM((REG, KB), F32),
            pltpu.VMEM((2, MX, KB), F32),
            pltpu.VMEM((2, MX, KB), F32),
            pltpu.VMEM((REG + 2, MX, 128), F32),
            pltpu.VMEM((REG + 2, M, 128), BF16),
            pltpu.VMEM((GROUP, M, 256), BF16),
            pltpu.VMEM((GROUP, M, 256), BF16),
            dma((2,)), dma((2,)), dma((2,)), dma((2,)), dma((3,)), dma((3,)), dma((3,)), dma((2,)),
        ],
        compiler_params=pltpu.CompilerParams(
            collective_id=0, has_side_effects=True, vmem_limit_bytes=48 * 2**20),
    )(st, w, y, pr, resample, blend)


UNROLL = 16
CHUNKS = 8


def analysis_kernel(s, t, near, weight, out, sv, tf, o, ov, s_sem, o_sem):
    step = COLS // CHUNKS

    def fetch(k):
        return pltpu.make_async_copy(
            s.at[pl.ds(k * step, step)], sv.at[pl.ds(k * step, step)], s_sem.at[k])

    for k in range(CHUNKS):
        fetch(k).start()
    base = lax.axis_index("space") * REG

    @pl.loop(0, REG + 2)
    def _(r):
        tf[r] = t[r].astype(F32)

    def column(c):
        beside = near[c] - base
        slot = jnp.where(beside < 0, REG, jnp.where(beside >= REG, REG + 1, (beside + 4) % REG))
        own = (c // WIDTH + 4) % REG
        share = weight[c]
        maps = (share * tf[own] + (1.0 - share) * tf[slot]).astype(BF16)
        o[c] = jnp.dot(sv[c, :, :M], maps, preferred_element_type=F32).astype(BF16)

    @pl.loop(0, CHUNKS)
    def _(k):
        fetch(k).wait()
        for i in range(step):
            column(k * step + i)

    def store(k):
        first = k * 16
        count = min(16, LEV - first)
        return pltpu.make_async_copy(
            ov.at[pl.ds(first, count)], out.at[pl.ds(first, count)], o_sem.at[k])

    for k in range(8):
        first, stop = k * 16, min(k * 16 + 16, LEV)
        turned = jnp.transpose(o[:, first : first + 16, :M], (1, 2, 0))
        ov[first:stop] = turned[: stop - first]
        store(k).start()
    for k in range(8):
        store(k).wait()


def analysis_call(s, t, near, weight):
    vmem = pl.BlockSpec(memory_space=pltpu.VMEM)
    hbm = pl.BlockSpec(memory_space=pl.ANY)
    smem = pl.BlockSpec(memory_space=pltpu.SMEM)
    return pl.pallas_call(
        analysis_kernel,
        out_shape=jax.ShapeDtypeStruct((LEV, M, COLS), BF16),
        in_specs=[hbm, vmem, smem, smem],
        out_specs=hbm,
        scratch_shapes=[
            pltpu.VMEM((COLS, 128, 128), BF16),
            pltpu.VMEM((REG + 2, M, 128), F32),
            pltpu.VMEM((COLS, 128, 128), BF16),
            pltpu.VMEM((LEV, M, COLS), BF16),
            pltpu.SemaphoreType.DMA((CHUNKS,)),
            pltpu.SemaphoreType.DMA((8,)),
        ],
        compiler_params=pltpu.CompilerParams(vmem_limit_bytes=48 * 2**20),
    )(s, t, near, weight)


def per_device(
    states, obs_weights, observations, obs_precision, resample_index, blend_weight,
    stencil_region, stencil_weight,
):
    st = jnp.transpose(states[0], (1, 0, 2))
    resample = jnp.pad(resample_index, ((0, 0), (0, 128 - M)), constant_values=-1)
    t, s = transforms_call(
        lax.axis_size("lag"), lax.axis_size("space"),
        st, obs_weights, observations, obs_precision, resample, blend_weight)
    out = analysis_call(s, t, stencil_region, stencil_weight)
    return jnp.transpose(out, (1, 0, 2))[None]


def solution(mesh):
    in_specs = (
        P("lag", None, None, "space"), P(), P(None, "space"), P(None, "space"),
        P("space", None), P("space"), P("space"), P("space"),
    )
    return jax.shard_map(
        per_device, mesh=mesh, in_specs=in_specs, out_specs=P("lag", None, None, "space"),
        check_vma=False)
```

profile of v0, /device:TPU:7, one launch (start us, length us, event | category | flops | bytes accessed | tf_op | source)
XLA Modules:
  0.0 55.7 jit_solution(9003145879293205681)
XLA Ops:
  0.0 0.0 copy-start.7
  0.0 0.0 copy-start.6
  0.0 0.7 %pad.4.resample = s32[16,128]{1,0:T(8,128)S(1)} pad(s32[16,80]{1,0:T(8,128)} %param.12, s32[]{:T(128)} %constant.0.clone.1), padding=0_0x0_48 | pad | bytes 13316 | tf_op jit(solution)/shard_map/jit(_pad)/pad | solution.py:427
  0.7 0.0 copy-start.1
  0.7 1.7 %copy-done.1 = bf16[1,80,127,128]{3,1,2,0:T(8,128)(2,1)S(1)} copy-done((bf16[1,80,127,128]{3,1,2,0:T(8,128)(2,1)S(1)}, bf16[1,80,127,128]{3,1,2,0:T(8,128)(2,1)}, u32[]{:S(2)}) %copy-start.1) | copy-done | bytes 2600984
  2.5 0.0 copy-start.2
  2.5 0.7 %copy-done.2 = f32[24,128]{1,0:T(8,128)S(1)} copy-done((f32[24,128]{1,0:T(8,128)S(1)}, f32[24,128]{1,0:T(8,128)}, u32[]{:S(2)}) %copy-start.2) | copy-done | bytes 12312
  3.2 0.0 copy-start.3
  3.2 0.7 %copy-done.3 = f32[24,128]{1,0:T(8,128)S(1)} copy-done((f32[24,128]{1,0:T(8,128)S(1)}, f32[24,128]{1,0:T(8,128)}, u32[]{:S(2)}) %copy-start.3) | copy-done | bytes 12312
  3.9 0.0 copy-start.4
  3.9 0.7 %copy-done.4 = bf16[24,127]{1,0:T(8,128)(2,1)S(1)} copy-done((bf16[24,127]{1,0:T(8,128)(2,1)S(1)}, bf16[24,127]{1,0:T(8,128)(2,1)}, u32[]{:S(2)}) %copy-start.4) | copy-done | bytes 6120
  4.6 0.0 copy-start.5
  4.6 0.7 %copy-done.5 = f32[16]{0:T(128)S(1)} copy-done((f32[16]{0:T(128)S(1)}, f32[16]{0:T(128)}, u32[]{:S(2)}) %copy-start.5) | copy-done | bytes 88
  5.2 41.1 %shard_map.82 = (bf16[18,80,128]{2,1,0:T(8,128)(2,1)S(1)}, bf16[128,128,128]{2,1,0:T(8,128)(2,1)}) custom-call(bf16[127,80,128]{2,1,0:T(8,128)(2,1)S(1)} %bitcast.6, bf16[24,127]{1,0:T(8,128)(2,1)S(1)} %copy-done.4, f32[24,128]{1,0:T(8,128)S(1)} %copy-done.2, f32[24,128]{1,0:T(8,128)S(1)} %copy-done.3, s32[16,128]{1,0:T(8,128)S(1)} %pad.4.resample, ...), custom_call_target="tpu_custom_call" | custom-call | tf_op jit(solution)/shard_map/pallas_call | solution.py:326
  46.4 0.0 copy-done.7
  46.4 0.0 copy-done.6
  46.4 0.0 copy-start
  46.4 2.2 %copy-done = bf16[128,128,128]{2,1,0:T(8,128)(2,1)S(1)} copy-done((bf16[128,128,128]{2,1,0:T(8,128)(2,1)S(1)}, bf16[128,128,128]{2,1,0:T(8,128)(2,1)}, u32[]{:S(2)}) %copy-start) | copy-done | bytes 4194328
  48.6 7.0 %shard_map.83 = bf16[127,80,128]{2,1,0:T(8,128)(2,1)} custom-call(bf16[128,128,128]{2,1,0:T(8,128)(2,1)S(1)} %copy-done, bf16[18,80,128]{2,1,0:T(8,128)(2,1)S(1)} %get-tuple-element.8.t, s32[128]{0:T(128)S(1)} %copy-done.6, f32[128]{0:T(128)S(1)} %copy-done.7), custom_call_target="tpu_custom_call" | custom-call | tf_op jit(solution)/shard_map/pallas_call | solution.py:405
Async XLA Ops:
  0.0 46.4 %copy-start.7 = (f32[128]{0:T(128)S(1)}, f32[128]{0:T(128)}, u32[]{:S(2)}) copy-start(f32[128]{0:T(128)} %weight.1) | copy-start | bytes 1540
  0.0 46.4 %copy-start.6 = (s32[128]{0:T(128)S(1)}, s32[128]{0:T(128)}, u32[]{:S(2)}) copy-start(s32[128]{0:T(128)} %near.1) | copy-start | bytes 1540
  0.7 1.7 %copy-start.1 = (bf16[1,80,127,128]{3,1,2,0:T(8,128)(2,1)S(1)}, bf16[1,80,127,128]{3,1,2,0:T(8,128)(2,1)}, u32[]{:S(2)}) copy-start(bf16[1,80,127,128]{3,1,2,0:T(8,128)(2,1)} %param.8) | copy-start | bytes 7802884
  2.5 0.7 %copy-start.2 = (f32[24,128]{1,0:T(8,128)S(1)}, f32[24,128]{1,0:T(8,128)}, u32[]{:S(2)}) copy-start(f32[24,128]{1,0:T(8,128)} %y.3) | copy-start | bytes 36868
  3.2 0.7 %copy-start.3 = (f32[24,128]{1,0:T(8,128)S(1)}, f32[24,128]{1,0:T(8,128)}, u32[]{:S(2)}) copy-start(f32[24,128]{1,0:T(8,128)} %pr.1) | copy-start | bytes 36868
  3.9 0.7 %copy-start.4 = (bf16[24,127]{1,0:T(8,128)(2,1)S(1)}, bf16[24,127]{1,0:T(8,128)(2,1)}, u32[]{:S(2)}) copy-start(bf16[24,127]{1,0:T(8,128)(2,1)} %w.1) | copy-start | bytes 18292
  4.6 0.7 %copy-start.5 = (f32[16]{0:T(128)S(1)}, f32[16]{0:T(128)}, u32[]{:S(2)}) copy-start(f32[16]{0:T(128)} %blend.1) | copy-start | bytes 196
  46.4 2.2 %copy-start = (bf16[128,128,128]{2,1,0:T(8,128)(2,1)S(1)}, bf16[128,128,128]{2,1,0:T(8,128)(2,1)}, u32[]{:S(2)}) copy-start(bf16[128,128,128]{2,1,0:T(8,128)(2,1)} %get-tuple-element.7.s) | copy-start | bytes 12582916
where the time goes:
time: 56.1 us; the launch traced here: 55.7 us
  Pallas kernels  48.1 us (86%)
  local copies, waits for them, and re-layouts  7.41 us (13%)
    pallas_call x1, Pallas kernels, transforms_call(): pl.pallas_call(make_transform_kernel(lags, spaces), out_shape=(jax.ShapeD...  41.1 us
    pallas_call x1, Pallas kernels, analysis_call(): pl.pallas_call(analysis_kernel, out_shape=jax.ShapeDtypeStruct((LEV, M, C...  6.98 us
    unnamed x16, local copies, waits for them, and re-layouts  6.68 us

commit v1 on v0

v1 whole, which is shorter than its diff:
```python
import math

import jax
import jax.numpy as jnp
from jax import lax
from jax.experimental import pallas as pl
from jax.experimental.pallas import tpu as pltpu
from jax.sharding import PartitionSpec as P

M = 80
LEV = 127
NOBS = 24
COLS = 128
WIDTH = 8
REG = 16
NS_ITERS = 8
KB = 256
MX = 96
UNROLL = 16
F32 = jnp.float32
BF16 = jnp.bfloat16
MESH = pl.DeviceIdType.MESH

TAPER = [
    [math.exp(-0.5 * ((q * WIDTH + k - (3 * WIDTH - 1) / 2.0) / WIDTH) ** 2) for k in range(WIDTH)]
    for q in range(3)
]


def split(x):
    high = x.astype(BF16)
    return high, (x - high.astype(F32)).astype(BF16)


def halves(x):
    high, low = split(x)
    return jnp.concatenate([high, low], axis=1)


def product(a, b):
    gap = jnp.zeros((128 - M, 256), BF16)
    out = jnp.dot(a, jnp.concatenate([b, gap, b, gap], axis=0), preferred_element_type=F32)
    return out[:, :128] + out[:, 128:]


def pair_rows(value, spread, chosen):
    first = value.astype(BF16)
    rest = value - first.astype(F32)
    second = rest.astype(BF16)
    third = (rest - second.astype(F32)).astype(BF16)
    dims = (((0,), (0,)), ((), ()))
    total = lax.dot_general(first, spread, dims, preferred_element_type=F32)
    total += lax.dot_general(second, spread, dims, preferred_element_type=F32)
    total += lax.dot_general(third, spread, dims, preferred_element_type=F32)
    return jnp.sum(jnp.where(chosen, total, 0.0).reshape(REG, WIDTH, KB), axis=1)


def prepare(w, y, pr, wb, yrow, rrow):
    row = lax.broadcasted_iota(jnp.int32, (NOBS, KB), 0)
    lane = lax.broadcasted_iota(jnp.int32, (NOBS, KB), 1)
    spread = jnp.where((lane % NOBS == row) & (lane < WIDTH * NOBS), 1.0, 0.0).astype(BF16)
    row = lax.broadcasted_iota(jnp.int32, (COLS, KB), 0)
    lane = lax.broadcasted_iota(jnp.int32, (COLS, KB), 1)
    chosen = lane // NOBS == row % WIDTH
    yrow[...] = pair_rows(y[...], spread, chosen)
    rrow[...] = pair_rows(jnp.sqrt(pr[...]), spread, chosen)
    wide = lax.dot_general(w[...], spread, (((0,), (0,)), ((), ())), preferred_element_type=F32)
    wide = jnp.concatenate([wide, jnp.zeros((1, KB), F32)], axis=0)
    for k in range(WIDTH):
        wb[k * 128 : (k + 1) * 128] = jnp.where(lane // NOBS == k, wide, 0.0).astype(BF16)


def scaled_blocks(regions, xc, wb, yrow, rrow):
    rows = []
    for r in regions:
        rows.append(jnp.concatenate([xc[r * WIDTH + k] for k in range(WIDTH)], axis=1))
    out = jnp.dot(jnp.concatenate(rows, axis=0), wb[...], preferred_element_type=F32)
    top = lax.broadcasted_iota(jnp.int32, (MX - M, KB), 0) == 0
    blocks = []
    for k, r in enumerate(regions):
        obs = out[k * M : (k + 1) * M]
        mean = jnp.sum(obs, axis=0, keepdims=True) * (1.0 / M)
        innovation = jnp.where(top, yrow[pl.ds(r, 1), :] - mean, 0.0)
        blocks.append(
            jnp.concatenate([obs - mean, innovation], axis=0) * rrow[pl.ds(r, 1), :]
        )
    return blocks


def gram_parts(x, parts):
    high, low = split(x)
    across = jnp.concatenate([x, jnp.zeros((128 - MX, KB), F32)], axis=0).T
    highs, lows = [], []
    for q in parts:
        tapered = [across[k * NOBS : (k + 1) * NOBS] * TAPER[q][k] for k in range(WIDTH)]
        h, l = split(jnp.concatenate(tapered, axis=0))
        highs.append(h)
        lows.append(l)
    used = WIDTH * NOBS
    n = 128 * len(parts)
    right = jnp.concatenate(highs + lows, axis=1)
    out = jnp.dot(high[:, :used], right, preferred_element_type=F32)
    out2 = jnp.dot(low[:, :used], right[:, :n], preferred_element_type=F32)
    total = out[:, :n] + out[:, n:] + out2
    return [total[:, k * 128 : (k + 1) * 128] for k in range(len(parts))]


def add_block(x, r, gram):
    parts = gram_parts(x, (0, 1, 2))
    gram[r + 2] += parts[0]
    gram[r + 1] += parts[1]
    gram[r] += parts[2]


def transforms_group(items, gram, ys, zs):
    row = lax.broadcasted_iota(jnp.int32, (M, 128), 0)
    col = lax.broadcasted_iota(jnp.int32, (M, 128), 1)
    eye = (row == col).astype(F32)
    count = len(items)
    norms = []
    for k, (slot, _, _) in enumerate(items):
        cross = jnp.where(col < M, gram[slot, :M, :], 0.0)
        square = jnp.sum(cross * cross, axis=0, keepdims=True)
        norm = 1.0 + jnp.sqrt(jnp.sum(square, axis=1, keepdims=True)) * (1.0 / (M - 1))
        norms.append(norm)
        y = (eye + cross * (1.0 / (M - 1))) / norm
        e = halves(1.5 * eye - 0.5 * y)
        ys[k] = halves(product(halves(y), e))
        zs[k] = e

    @pl.loop(0, NS_ITERS - 2)
    def _(sweep):
        factors = [halves(1.5 * eye - 0.5 * product(zs[k], ys[k])) for k in range(count)]
        for k in range(count):
            both = product(jnp.concatenate([ys[k], zs[k]], axis=0), factors[k])
            ys[k] = halves(both[:M])
            zs[k] = halves(both[M:])

    result = []
    for k, (slot, drawn_row, share) in enumerate(items):
        e = halves(1.5 * eye - 0.5 * product(zs[k], ys[k]))
        root = product(zs[k], e) / jnp.sqrt(norms[k])
        drive = gram[slot, :M, M : M + 1]
        half = jnp.sum(root * drive, axis=0, keepdims=True)
        mean_weight = jnp.sum(root * half, axis=1, keepdims=True) * (1.0 / (M - 1))
        weights = mean_weight + root
        etkf = 1.0 / M + weights - jnp.sum(weights, axis=0, keepdims=True) * (1.0 / M)
        drawn = (drawn_row == row).astype(F32)
        result.append((1.0 - share) * etkf + share * drawn)
    return result


def pack(maps):
    lane = lax.broadcasted_iota(jnp.int32, (M, 128), 1)
    a, b, c, d, e, f, g, h = maps

    def tail(first, second=None, cut=128):
        return first if second is None else jnp.where(lane < cut, first, second)

    spare = (
        pltpu.roll(f, 80, 1),
        tail(pltpu.roll(f, 32, 1), pltpu.roll(g, 112, 1), 112),
        pltpu.roll(g, 64, 1),
        tail(pltpu.roll(g, 16, 1), pltpu.roll(h, 96, 1), 96),
        pltpu.roll(h, 48, 1),
    )
    return [
        jnp.where(lane < M, kept, extra).astype(BF16)
        for kept, extra in zip((a, b, c, d, e), spare)
    ]


def unpack(slabs):
    lane = lax.broadcasted_iota(jnp.int32, (M, 128), 1)
    a, b, c, d, e = slabs
    f = jnp.where(lane < 48, pltpu.roll(a, 48, 1), pltpu.roll(b, 96, 1))
    g = jnp.where(
        lane < 16, pltpu.roll(b, 16, 1),
        jnp.where(lane < 64, pltpu.roll(c, 64, 1), pltpu.roll(d, 112, 1)))
    h = jnp.where(lane < 32, pltpu.roll(d, 32, 1), pltpu.roll(e, 80, 1))
    return [a, b, c, d, e, f, g, h]


ODD_REGIONS = (12, 13, 14, 15, 0, 1, 2, 3, -1, 16)
EVEN_REGIONS = (4, 5, 6, 7, 8, 9, 10, 11)
SLABS = 12
ODD_PIECES = ((0, 2), (2, 2), (4, 3))
EVEN_PIECES = ((7, 2), (9, 2), (11, 1))
LEVEL_CHUNKS = ((0, 32), (32, 32), (64, 32), (96, 31))


def make_transform_kernel(lags, spaces):
    last = lags - 1

    def kernel(
        st_hbm, w_hbm, y_hbm, pr_hbm, resample_hbm, blend_hbm, t_out, sc,
        st, w, y, pr, resample, blend,
        xc, wb, yrow, rrow, edge, halo, gram, t, ys, zs,
        in_sem, st_sem, x_send, x_recv, g_send, g_recv,
        p_next, p_side, own_recv, other_recv, ready,
    ):
        lag = lax.axis_index("lag")
        here = lax.axis_index("space")
        odd = lax.rem(lag, 2)
        sibling = lag + 1 - 2 * odd
        has_left, has_right = here > 0, here < spaces - 1
        left, right = here - 1, here + 1
        barrier = pltpu.get_barrier_semaphore()
        is_last = lag == last

        def greet(where):
            pl.semaphore_signal(barrier, inc=1, device_id=where, device_id_type=MESH)

        greet({"lag": sibling})

        @pl.when(lag >= 2)
        def _():
            greet({"lag": lag - 2})

        @pl.when(is_last)
        def _():
            @pl.when(has_left)
            def _():
                greet({"space": left})

            @pl.when(has_right)
            def _():
                greet({"space": right})

        def level_copy(k):
            first, count = LEVEL_CHUNKS[k]
            return pltpu.make_async_copy(
                st_hbm.at[pl.ds(first, count)], st.at[pl.ds(first, count)], st_sem.at[k])

        small = [
            pltpu.make_async_copy(src, dst, in_sem.at[k])
            for k, (src, dst) in enumerate(
                ((w_hbm, w), (y_hbm, y), (pr_hbm, pr), (resample_hbm, resample), (blend_hbm, blend)))
        ]
        for copy in small:
            copy.start()
        for k in range(len(LEVEL_CHUNKS)):
            level_copy(k).start()
        for copy in small:
            copy.wait()

        def columns_first():
            for k in range(0, 128, 16):
                stop = min(k + 16, LEV)
                sc[:, k:stop, :M] = jnp.transpose(st[k:stop], (2, 0, 1))

        def side(k, pieces):
            ref = t.at[pl.ds(*pieces[k])]
            return pltpu.make_async_remote_copy(
                src_ref=ref, dst_ref=ref, send_sem=p_side.at[k], recv_sem=other_recv.at[k],
                device_id={"lag": sibling}, device_id_type=MESH)

        def onward(k, pieces):
            ref = t.at[pl.ds(*pieces[k])]
            return pltpu.make_async_remote_copy(
                src_ref=ref, dst_ref=ref, send_sem=p_next.at[k], recv_sem=own_recv.at[k],
                device_id={"lag": lag - 2}, device_id_type=MESH)

        def block_copy(k, where):
            return pltpu.make_async_remote_copy(
                src_ref=edge.at[k], dst_ref=halo.at[1 - k], send_sem=x_send.at[k],
                recv_sem=x_recv.at[1 - k], device_id={"space": where}, device_id_type=MESH)

        def gram_copy():
            ref = gram.at[pl.ds(5, 8)]
            return pltpu.make_async_remote_copy(
                src_ref=ref, dst_ref=ref, send_sem=g_send, recv_sem=g_recv,
                device_id={"lag": sibling}, device_id_type=MESH)

        def drawn_row(r):
            return resample[r : r + 1, :]

        def wide_row(r):
            return jnp.concatenate([drawn_row(r), jnp.full((1, 48), -1, jnp.int32)], axis=1)

        def item(r):
            return (r + 1, wide_row(r), blend[r])

        def with_extras(x, r):
            values = jnp.concatenate(
                [drawn_row(r).astype(F32), jnp.zeros((1, KB - M), F32)], axis=1)
            which = lax.broadcasted_iota(jnp.int32, (MX, KB), 0)
            return jnp.where(which == M + 1, values, jnp.where(which == M + 2, blend[r], x))

        def outside_item(k, slot):
            drawn = halo[k, 0, M + 1 : M + 2, :128].astype(jnp.int32)
            return (slot, drawn, halo[k, 0, M + 2 : M + 3, :128])

        sides = ((0, has_left, left), (1, has_right, right))

        @pl.when(is_last)
        def _():
            prepare(w, y, pr, wb, yrow, rrow)

            @pl.loop(0, REG + 2)
            def _(r):
                gram[r] = jnp.zeros((MX, 128), F32)

            for k in range(len(LEVEL_CHUNKS)):
                level_copy(k).wait()
            xc[...] = jnp.transpose(
                jnp.concatenate([st[...], jnp.zeros((1, M, COLS), BF16)], axis=0), (2, 1, 0))

            ends = scaled_blocks((0, 1, REG - 1, REG - 2), xc, wb, yrow, rrow)
            edge[0, 0], edge[0, 1] = with_extras(ends[0], 0), ends[1]
            edge[1, 0], edge[1, 1] = with_extras(ends[2], REG - 1), ends[3]
            pl.semaphore_wait(
                barrier, 1 + has_left.astype(jnp.int32) + has_right.astype(jnp.int32))
            for k, there, where in sides:
                @pl.when(there)
                def _(k=k, where=where):
                    block_copy(k, where).start()

            @pl.loop(0, 5)
            def _(i):
                pair = (3 + 2 * i, 4 + 2 * i)
                for r, x in zip(pair, scaled_blocks(pair, xc, wb, yrow, rrow)):
                    add_block(x, r, gram)

            gram_copy().start()
            for r, x in zip((2, 13), scaled_blocks((2, 13), xc, wb, yrow, rrow)):
                add_block(x, r, gram)
            for k, j, r in ((0, 0, 0), (0, 1, 1), (1, 0, REG - 1), (1, 1, REG - 2)):
                add_block(edge[k, j], r, gram)

            for k, there, where in sides:
                @pl.when(there)
                def _(k=k, where=where):
                    block_copy(1 - k, where).wait_recv()
                    block_copy(k, where).wait_send()

                @pl.when(jnp.logical_not(there))
                def _(k=k):
                    halo[k] = jnp.zeros((2, MX, KB), F32)
            near = gram_parts(halo[0, 0], (0, 1))
            gram[1] += near[0]
            gram[0] += near[1] + gram_parts(halo[0, 1], (0,))[0]
            near = gram_parts(halo[1, 0], (1, 2))
            gram[REG] += near[1]
            gram[REG + 1] += near[0] + gram_parts(halo[1, 1], (2,))[0]

            items = [item(r) for r in ODD_REGIONS[:8]]
            items += [outside_item(0, 0), outside_item(1, REG + 1)]
            maps = transforms_group(items, gram, ys, zs)
            for k, slab in enumerate(pack(maps[:8]) + [m.astype(BF16) for m in maps[8:]]):
                t[k] = slab
            gram_copy().wait_send()

        @pl.when(jnp.logical_not(is_last))
        def _():
            for k in range(len(LEVEL_CHUNKS)):
                level_copy(k).wait()
            columns_first()
            pl.semaphore_wait(barrier, 1 + (lag < last - 1).astype(jnp.int32))

            @pl.when(lag < last - 1)
            def _():
                pl.semaphore_signal(
                    ready, inc=1, device_id={"lag": lag + 2}, device_id_type=MESH)

        @pl.when(lag == last - 1)
        def _():
            gram_copy().wait_recv()
            maps = transforms_group([item(r) for r in EVEN_REGIONS], gram, ys, zs)
            for k, slab in enumerate(pack(maps)):
                t[7 + k] = slab

        @pl.when(lag >= 2)
        def _():
            pl.semaphore_wait(ready, 1)

        for parity, own, other in ((1, ODD_PIECES, EVEN_PIECES), (0, EVEN_PIECES, ODD_PIECES)):
            @pl.when(odd == parity)
            def _(own=own, other=other):
                for k in range(3):
                    @pl.when(lag < last - 1)
                    def _(k=k):
                        onward(k, own).wait_recv()

                    side(k, own).start()

                    @pl.when(lag >= 2)
                    def _(k=k):
                        onward(k, own).start()

                @pl.when(is_last)
                def _():
                    columns_first()

                for k in range(3):
                    side(k, other).wait_recv()
                for k in range(3):
                    side(k, own).wait_send()

                    @pl.when(lag >= 2)
                    def _(k=k):
                        onward(k, own).wait_send()

        t_out[...] = t[...]

    return kernel


def transforms_call(lags, spaces, st, w, y, pr, resample, blend):
    vmem = pl.BlockSpec(memory_space=pltpu.VMEM)
    hbm = pl.BlockSpec(memory_space=pltpu.HBM)
    dma = pltpu.SemaphoreType.DMA
    return pl.pallas_call(
        make_transform_kernel(lags, spaces),
        out_shape=(
            jax.ShapeDtypeStruct((SLABS, M, 128), BF16),
            jax.ShapeDtypeStruct((COLS, 128, 128), BF16),
        ),
        in_specs=[hbm] * 6,
        out_specs=(vmem, vmem),
        scratch_shapes=[
            pltpu.VMEM((LEV, M, COLS), BF16),
            pltpu.VMEM((NOBS, LEV), BF16),
            pltpu.VMEM((NOBS, COLS), F32),
            pltpu.VMEM((NOBS, COLS), F32),
            pltpu.VMEM((REG, M), jnp.int32),
            pltpu.SMEM((REG,), F32),
            pltpu.VMEM((COLS, M, 128), BF16),
            pltpu.VMEM((WIDTH * 128, KB), BF16),
            pltpu.VMEM((REG, KB), F32),
            pltpu.VMEM((REG, KB), F32),
            pltpu.VMEM((2, 2, MX, KB), F32),
            pltpu.VMEM((2, 2, MX, KB), F32),
            pltpu.VMEM((REG + 2, MX, 128), F32),
            pltpu.VMEM((SLABS, M, 128), BF16),
            pltpu.VMEM((10, M, 256), BF16),
            pltpu.VMEM((10, M, 256), BF16),
            dma((5,)), dma((4,)), dma((2,)), dma((2,)), dma, dma,
            dma((3,)), dma((3,)), dma((3,)), dma((3,)), pltpu.SemaphoreType.REGULAR,
        ],
        compiler_params=pltpu.CompilerParams(
            collective_id=0, has_side_effects=True, vmem_limit_bytes=24 * 2**20),
    )(*(pltpu.with_memory_space_constraint(x, pltpu.HBM) for x in (st, w, y, pr, resample, blend)))


def analysis_kernel(s, t, near, weight, out, tf, o, ov, o_sem):
    base = lax.axis_index("space") * REG - 1
    slabs = [t[k].astype(F32) for k in range(SLABS)]
    maps = unpack(slabs[:5]) + slabs[5:7] + unpack(slabs[7:])
    for r, m in zip(ODD_REGIONS + EVEN_REGIONS, maps):
        tf[r + 1] = m

    def column(c):
        share = weight[c]
        maps = (share * tf[c // WIDTH + 1] + (1.0 - share) * tf[near[c] - base]).astype(BF16)
        o[c] = jnp.dot(s[c, :, :M], maps, preferred_element_type=F32).astype(BF16)

    @pl.loop(0, COLS, step=UNROLL)
    def _(first):
        for i in range(UNROLL):
            column(first + i)

    def store(k):
        first = k * 16
        count = min(16, LEV - first)
        return pltpu.make_async_copy(
            ov.at[pl.ds(first, count)], out.at[pl.ds(first, count)], o_sem.at[k])

    for k in range(8):
        first, stop = k * 16, min(k * 16 + 16, LEV)
        turned = jnp.transpose(o[:, first : first + 16, :M], (1, 2, 0))
        ov[first:stop] = turned[: stop - first]
        store(k).start()
    for k in range(8):
        store(k).wait()


def analysis_call(s, t, near, weight):
    vmem = pl.BlockSpec(memory_space=pltpu.VMEM)
    hbm = pl.BlockSpec(memory_space=pltpu.HBM)
    smem = pl.BlockSpec(memory_space=pltpu.SMEM)
    return pl.pallas_call(
        analysis_kernel,
        out_shape=jax.ShapeDtypeStruct((LEV, M, COLS), BF16),
        in_specs=[vmem, vmem, smem, smem],
        out_specs=hbm,
        scratch_shapes=[
            pltpu.VMEM((REG + 2, M, 128), F32),
            pltpu.VMEM((COLS, 128, 128), BF16),
            pltpu.VMEM((LEV, M, COLS), BF16),
            pltpu.SemaphoreType.DMA((8,)),
        ],
        compiler_params=pltpu.CompilerParams(vmem_limit_bytes=24 * 2**20),
    )(s, t, near, weight)


def per_device(
    states, obs_weights, observations, obs_precision, resample_index, blend_weight,
    stencil_region, stencil_weight,
):
    st = jnp.transpose(states[0], (1, 0, 2))
    t, s = transforms_call(
        lax.axis_size("lag"), lax.axis_size("space"),
        st, obs_weights, observations, obs_precision, resample_index, blend_weight)
    out = analysis_call(s, t, stencil_region, stencil_weight)
    return jnp.transpose(out, (1, 0, 2))[None]


def solution(mesh):
    in_specs = (
        P("lag", None, None, "space"), P(), P(None, "space"), P(None, "space"),
        P("space", None), P("space"), P("space"), P("space"),
    )
    return jax.shard_map(
        per_device, mesh=mesh, in_specs=in_specs, out_specs=P("lag", None, None, "space"),
        check_vma=False)
```

time: 56.1 us -> 41.9 us (0.75)
  local copies, waits for them, and re-layouts: 7.41 us -> 0.01 us
  Pallas kernels: 48.1 us -> 41.5 us
    unnamed x16 -> x4, local copies, waits for them, and re-layouts: 6.68 us -> 0.01 us
    pallas_call x1, Pallas kernels: 41.1 us -> 35.6 us  [transforms_call(): pl.pallas_call(make_transform_kernel(lags, spaces), out_shape=(jax.ShapeD...]
    pallas_call x1, Pallas kernels: 6.98 us -> 5.97 us  [analysis_call(): pl.pallas_call(analysis_kernel, out_shape=jax.ShapeDtypeStruct((LEV, M, C...]
    pad x1 -> x0, local copies, waits for them, and re-layouts: 0.73 us -> none  [per_device(): jnp.pad(resample_index, ((0, 0), (0, 128 - M)), constant_values=-1)]
where the time goes in v1:
time: 41.9 us; the launch traced here: 41.7 us
  Pallas kernels  41.5 us (99%)
    pallas_call x1, Pallas kernels, transforms_call(): pl.pallas_call(make_transform_kernel(lags, spaces), out_shape=(jax.ShapeD...  35.6 us
    pallas_call x1, Pallas kernels, analysis_call(): pl.pallas_call(analysis_kernel, out_shape=jax.ShapeDtypeStruct((LEV, M, C...  5.97 us

profile of v1, /device:TPU:7, one launch (start us, length us, event | category | flops | bytes accessed | tf_op | source)
XLA Modules:
  0.0 41.7 jit_solution(514432160463151896)
XLA Ops:
  0.0 0.0 copy-start.1
  0.0 0.0 copy-start
  0.0 35.6 %shard_map.82 = (bf16[12,80,128]{2,1,0:T(8,128)(2,1)S(1)}, bf16[128,128,128]{2,1,0:T(8,128)(2,1)S(1)}) custom-call(bf16[127,80,128]{2,1,0:T(8,128)(2,1)} %bitcast.6, bf16[24,127]{1,0:T(8,128)(2,1)} %w_hbm.1, f32[24,128]{1,0:T(8,128)} %y_hbm.1, f32[24,128]{1,0:T(8,128)} %pr_hbm.1, s32[16,80]{1,0:T(8,128)} %resample_hbm.1, f32[16]{0:T(128)} %blend_hbm.1), custom_call_target="tpu_custom_call" | custom-call | tf_op jit(solution)/shard_map/pallas_call | solution.py:413
  35.6 0.0 copy-done.1
  35.6 0.0 copy-done
  35.6 6.0 %shard_map.83 = bf16[127,80,128]{2,1,0:T(8,128)(2,1)} custom-call(bf16[128,128,128]{2,1,0:T(8,128)(2,1)S(1)} %get-tuple-element.7.s, bf16[12,80,128]{2,1,0:T(8,128)(2,1)S(1)} %get-tuple-element.8.t, s32[128]{0:T(128)S(1)} %copy-done, f32[128]{0:T(128)S(1)} %copy-done.1), custom_call_target="tpu_custom_call" | custom-call | tf_op jit(solution)/shard_map/pallas_call | solution.py:482
Async XLA Ops:
  0.0 35.6 %copy-start.1 = (f32[128]{0:T(128)S(1)}, f32[128]{0:T(128)}, u32[]{:S(2)}) copy-start(f32[128]{0:T(128)} %weight.1) | copy-start | bytes 1540
  0.0 35.6 %copy-start = (s32[128]{0:T(128)S(1)}, s32[128]{0:T(128)}, u32[]{:S(2)}) copy-start(s32[128]{0:T(128)} %near.1) | copy-start | bytes 1540

commit v2 on v1

--- a/solution.py
+++ b/solution.py
@@ -16,7 +16,6 @@
 NS_ITERS = 8
 KB = 256
 MX = 96
-UNROLL = 16
 F32 = jnp.float32
 BF16 = jnp.bfloat16
 MESH = pl.DeviceIdType.MESH
@@ -70,10 +69,11 @@
         wb[k * 128 : (k + 1) * 128] = jnp.where(lane // NOBS == k, wide, 0.0).astype(BF16)
 
 
-def scaled_blocks(regions, xc, wb, yrow, rrow):
+def scaled_blocks(regions, sc, wb, yrow, rrow):
     rows = []
     for r in regions:
-        rows.append(jnp.concatenate([xc[r * WIDTH + k] for k in range(WIDTH)], axis=1))
+        turned = jnp.transpose(sc[pl.ds(r * WIDTH, WIDTH)], (0, 2, 1))[:, :M]
+        rows.append(jnp.concatenate([turned[k] for k in range(WIDTH)], axis=1))
     out = jnp.dot(jnp.concatenate(rows, axis=0), wb[...], preferred_element_type=F32)
     top = lax.broadcasted_iota(jnp.int32, (MX - M, KB), 0) == 0
     blocks = []
@@ -87,29 +87,27 @@
     return blocks
 
 
-def gram_parts(x, parts):
-    high, low = split(x)
+def block_terms(x, parts):
+    left = split(x)
     across = jnp.concatenate([x, jnp.zeros((128 - MX, KB), F32)], axis=0).T
-    highs, lows = [], []
+    gap = jnp.zeros((KB - WIDTH * NOBS, 128), F32)
+    terms = {}
     for q in parts:
         tapered = [across[k * NOBS : (k + 1) * NOBS] * TAPER[q][k] for k in range(WIDTH)]
-        h, l = split(jnp.concatenate(tapered, axis=0))
-        highs.append(h)
-        lows.append(l)
-    used = WIDTH * NOBS
-    n = 128 * len(parts)
-    right = jnp.concatenate(highs + lows, axis=1)
-    out = jnp.dot(high[:, :used], right, preferred_element_type=F32)
-    out2 = jnp.dot(low[:, :used], right[:, :n], preferred_element_type=F32)
-    total = out[:, :n] + out[:, n:] + out2
-    return [total[:, k * 128 : (k + 1) * 128] for k in range(len(parts))]
-
-
-def add_block(x, r, gram):
-    parts = gram_parts(x, (0, 1, 2))
-    gram[r + 2] += parts[0]
-    gram[r + 1] += parts[1]
-    gram[r] += parts[2]
+        terms[q] = (*left, halves(jnp.concatenate(tapered + [gap], axis=0)))
+    return terms
+
+
+def gram_of(terms):
+    high, low, right = zip(*terms)
+    right = jnp.concatenate(right, axis=0)
+    out = jnp.dot(jnp.concatenate(high, axis=1), right, preferred_element_type=F32)
+    out2 = jnp.dot(jnp.concatenate(low, axis=1), right[:, :128], preferred_element_type=F32)
+    return out[:, :128] + out[:, 128:] + out2
+
+
+def region_gram(r, blocks):
+    return gram_of([blocks[r - 1 + q][q] for q in range(3)])
 
 
 def transforms_group(items, gram, ys, zs):
@@ -195,7 +193,7 @@
     def kernel(
         st_hbm, w_hbm, y_hbm, pr_hbm, resample_hbm, blend_hbm, t_out, sc,
         st, w, y, pr, resample, blend,
-        xc, wb, yrow, rrow, edge, halo, gram, t, ys, zs,
+        wb, yrow, rrow, edge, halo, gram, t, ys, zs,
         in_sem, st_sem, x_send, x_recv, g_send, g_recv,
         p_next, p_side, own_recv, other_recv, ready,
     ):
@@ -245,9 +243,14 @@
             copy.wait()
 
         def columns_first():
-            for k in range(0, 128, 16):
-                stop = min(k + 16, LEV)
-                sc[:, k:stop, :M] = jnp.transpose(st[k:stop], (2, 0, 1))
+            gap = jnp.zeros((1, M, COLS), BF16)
+            for k, (first, count) in enumerate(LEVEL_CHUNKS):
+                level_copy(k).wait()
+                for j in range(first, first + count, 16):
+                    part = st[j : min(j + 16, LEV)]
+                    if j + 16 > LEV:
+                        part = jnp.concatenate([part, gap], axis=0)
+                    sc[:, j : j + 16, :M] = jnp.transpose(part, (2, 0, 1))
 
         def side(k, pieces):
             ref = t.at[pl.ds(*pieces[k])]
@@ -293,20 +296,13 @@
 
         sides = ((0, has_left, left), (1, has_right, right))
 
+        columns_first()
+
         @pl.when(is_last)
         def _():
             prepare(w, y, pr, wb, yrow, rrow)
 
-            @pl.loop(0, REG + 2)
-            def _(r):
-                gram[r] = jnp.zeros((MX, 128), F32)
-
-            for k in range(len(LEVEL_CHUNKS)):
-                level_copy(k).wait()
-            xc[...] = jnp.transpose(
-                jnp.concatenate([st[...], jnp.zeros((1, M, COLS), BF16)], axis=0), (2, 1, 0))
-
-            ends = scaled_blocks((0, 1, REG - 1, REG - 2), xc, wb, yrow, rrow)
+            ends = scaled_blocks((0, 1, REG - 1, REG - 2), sc, wb, yrow, rrow)
             edge[0, 0], edge[0, 1] = with_extras(ends[0], 0), ends[1]
             edge[1, 0], edge[1, 1] = with_extras(ends[2], REG - 1), ends[3]
             pl.semaphore_wait(
@@ -316,17 +312,19 @@
                 def _(k=k, where=where):
                     block_copy(k, where).start()
 
-            @pl.loop(0, 5)
-            def _(i):
-                pair = (3 + 2 * i, 4 + 2 * i)
-                for r, x in zip(pair, scaled_blocks(pair, xc, wb, yrow, rrow)):
-                    add_block(x, r, gram)
-
+            inner = tuple(range(3, 13))
+            blocks = {}
+            for r, x in zip(inner, scaled_blocks(inner, sc, wb, yrow, rrow)):
+                blocks[r] = block_terms(x, (0, 1, 2))
+            for r in EVEN_REGIONS:
+                gram[r + 1] = region_gram(r, blocks)
             gram_copy().start()
-            for r, x in zip((2, 13), scaled_blocks((2, 13), xc, wb, yrow, rrow)):
-                add_block(x, r, gram)
-            for k, j, r in ((0, 0, 0), (0, 1, 1), (1, 0, REG - 1), (1, 1, REG - 2)):
-                add_block(edge[k, j], r, gram)
+            for r, x in zip((2, 13), scaled_blocks((2, 13), sc, wb, yrow, rrow)):
+                blocks[r] = block_terms(x, (0, 1, 2))
+            for r, x in zip((0, 1, 15, 14), ends):
+                blocks[r] = block_terms(x, (0, 1, 2))
+            for r in (1, 2, 3, 12, 13, 14):
+                gram[r + 1] = region_gram(r, blocks)
 
             for k, there, where in sides:
                 @pl.when(there)
@@ -337,12 +335,12 @@
                 @pl.when(jnp.logical_not(there))
                 def _(k=k):
                     halo[k] = jnp.zeros((2, MX, KB), F32)
-            near = gram_parts(halo[0, 0], (0, 1))
-            gram[1] += near[0]
-            gram[0] += near[1] + gram_parts(halo[0, 1], (0,))[0]
-            near = gram_parts(halo[1, 0], (1, 2))
-            gram[REG] += near[1]
-            gram[REG + 1] += near[0] + gram_parts(halo[1, 1], (2,))[0]
+            blocks[-1] = block_terms(halo[0, 0], (0, 1))
+            blocks[-2] = block_terms(halo[0, 1], (0,))
+            blocks[16] = block_terms(halo[1, 0], (1, 2))
+            blocks[17] = block_terms(halo[1, 1], (2,))
+            for r in (-1, 0, 15, 16):
+                gram[r + 1] = region_gram(r, blocks)
 
             items = [item(r) for r in ODD_REGIONS[:8]]
             items += [outside_item(0, 0), outside_item(1, REG + 1)]
@@ -353,9 +351,6 @@
 
         @pl.when(jnp.logical_not(is_last))
         def _():
-            for k in range(len(LEVEL_CHUNKS)):
-                level_copy(k).wait()
-            columns_first()
             pl.semaphore_wait(barrier, 1 + (lag < last - 1).astype(jnp.int32))
 
             @pl.when(lag < last - 1)
@@ -387,10 +382,6 @@
                     @pl.when(lag >= 2)
                     def _(k=k):
                         onward(k, own).start()
-
-                @pl.when(is_last)
-                def _():
-                    columns_first()
 
                 for k in range(3):
                     side(k, other).wait_recv()
@@ -425,7 +416,6 @@
             pltpu.VMEM((NOBS, COLS), F32),
             pltpu.VMEM((REG, M), jnp.int32),
             pltpu.SMEM((REG,), F32),
-            pltpu.VMEM((COLS, M, 128), BF16),
             pltpu.VMEM((WIDTH * 128, KB), BF16),
             pltpu.VMEM((REG, KB), F32),
             pltpu.VMEM((REG, KB), F32),
@@ -455,10 +445,8 @@
         maps = (share * tf[c // WIDTH + 1] + (1.0 - share) * tf[near[c] - base]).astype(BF16)
         o[c] = jnp.dot(s[c, :, :M], maps, preferred_element_type=F32).astype(BF16)
 
-    @pl.loop(0, COLS, step=UNROLL)
-    def _(first):
-        for i in range(UNROLL):
-            column(first + i)
+    for c in range(COLS):
+        column(c)
 
     def store(k):
         first = k * 16

time: 41.9 us -> 40.8 us (0.974)
  Pallas kernels: 41.5 us -> 40.5 us
    pallas_call x1, Pallas kernels: 5.97 us -> 4.77 us  [analysis_call(): pl.pallas_call(analysis_kernel, out_shape=jax.ShapeDtypeStruct((LEV, M, C...]
where the time goes in v2:
time: 40.8 us; the launch traced here: 40.7 us
  Pallas kernels  40.5 us (99%)
    pallas_call x1, Pallas kernels, transforms_call(): pl.pallas_call(make_transform_kernel(lags, spaces), out_shape=(jax.ShapeD...  35.7 us
    pallas_call x1, Pallas kernels, analysis_call(): pl.pallas_call(analysis_kernel, out_shape=jax.ShapeDtypeStruct((LEV, M, C...  4.77 us

profile of v2, /device:TPU:7, one launch (start us, length us, event | category | flops | bytes accessed | tf_op | source)
XLA Modules:
  0.0 40.7 jit_solution(12078912067392432331)
XLA Ops:
  0.0 0.0 copy-start.1
  0.0 0.0 copy-start
  0.0 35.7 %shard_map.82 = (bf16[12,80,128]{2,1,0:T(8,128)(2,1)S(1)}, bf16[128,128,128]{2,1,0:T(8,128)(2,1)S(1)}) custom-call(bf16[127,80,128]{2,1,0:T(8,128)(2,1)} %bitcast.6, bf16[24,127]{1,0:T(8,128)(2,1)} %w_hbm.1, f32[24,128]{1,0:T(8,128)} %y_hbm.1, f32[24,128]{1,0:T(8,128)} %pr_hbm.1, s32[16,80]{1,0:T(8,128)} %resample_hbm.1, f32[16]{0:T(128)} %blend_hbm.1), custom_call_target="tpu_custom_call" | custom-call | tf_op jit(solution)/shard_map/pallas_call | solution.py:404
  35.7 0.0 copy-done.1
  35.7 0.0 copy-done
  35.7 4.8 %shard_map.83 = bf16[127,80,128]{2,1,0:T(8,128)(2,1)} custom-call(bf16[128,128,128]{2,1,0:T(8,128)(2,1)S(1)} %get-tuple-element.7.s, bf16[12,80,128]{2,1,0:T(8,128)(2,1)S(1)} %get-tuple-element.8.t, s32[128]{0:T(128)S(1)} %copy-done, f32[128]{0:T(128)S(1)} %copy-done.1), custom_call_target="tpu_custom_call" | custom-call | tf_op jit(solution)/shard_map/pallas_call | solution.py:470
Async XLA Ops:
  0.0 35.7 %copy-start.1 = (f32[128]{0:T(128)S(1)}, f32[128]{0:T(128)}, u32[]{:S(2)}) copy-start(f32[128]{0:T(128)} %weight.1) | copy-start | bytes 1540
  0.0 35.7 %copy-start = (s32[128]{0:T(128)S(1)}, s32[128]{0:T(128)}, u32[]{:S(2)}) copy-start(s32[128]{0:T(128)} %near.1) | copy-start | bytes 1540

commit v3 on v2

--- a/solution.py
+++ b/solution.py
@@ -179,11 +179,11 @@
     return [a, b, c, d, e, f, g, h]
 
 
-ODD_REGIONS = (12, 13, 14, 15, 0, 1, 2, 3, -1, 16)
+ODD_REGIONS = (12, 13, 14, 15, 16, 1, 2, 3)
+LATE_REGIONS = (-1, 0)
 EVEN_REGIONS = (4, 5, 6, 7, 8, 9, 10, 11)
 SLABS = 12
-ODD_PIECES = ((0, 2), (2, 2), (4, 3))
-EVEN_PIECES = ((7, 2), (9, 2), (11, 1))
+PIECES = ((0, 3), (3, 2))
 LEVEL_CHUNKS = ((0, 32), (32, 32), (64, 32), (96, 31))
 
 
@@ -195,7 +195,7 @@
         st, w, y, pr, resample, blend,
         wb, yrow, rrow, edge, halo, gram, t, ys, zs,
         in_sem, st_sem, x_send, x_recv, g_send, g_recv,
-        p_next, p_side, own_recv, other_recv, ready,
+        p_next, p_side, own_recv, other_recv, f_send, f_recv, ready,
     ):
         lag = lax.axis_index("lag")
         here = lax.axis_index("space")
@@ -211,9 +211,10 @@
 
         greet({"lag": sibling})
 
-        @pl.when(lag >= 2)
+        @pl.when(lag >= last - 1)
         def _():
-            greet({"lag": lag - 2})
+            for back in (6, 4, 2):
+                greet({"lag": lag - back})
 
         @pl.when(is_last)
         def _():
@@ -252,17 +253,41 @@
                         part = jnp.concatenate([part, gap], axis=0)
                     sc[:, j : j + 16, :M] = jnp.transpose(part, (2, 0, 1))
 
-        def side(k, pieces):
-            ref = t.at[pl.ds(*pieces[k])]
+        def side(k, first):
+            ref = t.at[pl.ds(first + PIECES[k][0], PIECES[k][1])]
             return pltpu.make_async_remote_copy(
                 src_ref=ref, dst_ref=ref, send_sem=p_side.at[k], recv_sem=other_recv.at[k],
                 device_id={"lag": sibling}, device_id_type=MESH)
 
-        def onward(k, pieces):
-            ref = t.at[pl.ds(*pieces[k])]
+        def direct(k, first, back):
+            ref = t.at[pl.ds(first + PIECES[k][0], PIECES[k][1])]
             return pltpu.make_async_remote_copy(
-                src_ref=ref, dst_ref=ref, send_sem=p_next.at[k], recv_sem=own_recv.at[k],
-                device_id={"lag": lag - 2}, device_id_type=MESH)
+                src_ref=ref, dst_ref=ref, send_sem=p_next.at[k, back // 2 - 1],
+                recv_sem=own_recv.at[k], device_id={"lag": lag - back}, device_id_type=MESH)
+
+        def late(back):
+            ref = t.at[pl.ds(5, 2)]
+            return pltpu.make_async_remote_copy(
+                src_ref=ref, dst_ref=ref, send_sem=f_send.at[back // 2], recv_sem=f_recv,
+                device_id={"lag": lag - back}, device_id_type=MESH)
+
+        def each_direct(first, act):
+            for back in (6, 4, 2):
+                for k in range(len(PIECES)):
+                    act(direct(k, first, back))
+
+        def each_side(first, act):
+            for k in range(len(PIECES)):
+                act(side(k, first))
+
+        def start(copy):
+            copy.start()
+
+        def sent(copy):
+            copy.wait_send()
+
+        def arrived(copy):
+            copy.wait_recv()
 
         def block_copy(k, where):
             return pltpu.make_async_remote_copy(
@@ -284,27 +309,55 @@
         def item(r):
             return (r + 1, wide_row(r), blend[r])
 
-        def with_extras(x, r):
+        def payload(near, far, r):
             values = jnp.concatenate(
                 [drawn_row(r).astype(F32), jnp.zeros((1, KB - M), F32)], axis=1)
-            which = lax.broadcasted_iota(jnp.int32, (MX, KB), 0)
-            return jnp.where(which == M + 1, values, jnp.where(which == M + 2, blend[r], x))
+            which = lax.broadcasted_iota(jnp.int32, (88, KB), 0)
+            near = jnp.where(
+                which == M + 1, values, jnp.where(which == M + 2, blend[r], near[:88]))
+            lane = lax.broadcasted_iota(jnp.int32, (88, 128), 1)
+            both = jnp.where(lane < 64, near[:, 128:], pltpu.roll(far[:88, 128:], 64, 1))
+            return jnp.concatenate([near[:, :128], both, far[:88, :128]], axis=1)
+
+        def received(k):
+            lane = lax.broadcasted_iota(jnp.int32, (88, 128), 1)
+            both = halo[k, :, 128:256]
+            near = jnp.concatenate([halo[k, :, :128], jnp.where(lane < 64, both, 0.0)], axis=1)
+            far = jnp.concatenate(
+                [halo[k, :, 256:], jnp.where(lane < 64, pltpu.roll(both, 64, 1), 0.0)], axis=1)
+            gap = jnp.zeros((MX - 88, KB), F32)
+            return (jnp.concatenate([near, gap], axis=0), jnp.concatenate([far, gap], axis=0))
+
+        def await_halo(k):
+            there, where = ((has_left, left), (has_right, right))[k]
+
+            @pl.when(there)
+            def _():
+                block_copy(1 - k, where).wait_recv()
+                block_copy(k, where).wait_send()
+
+            @pl.when(jnp.logical_not(there))
+            def _():
+                halo[k] = jnp.zeros((88, 384), F32)
 
         def outside_item(k, slot):
-            drawn = halo[k, 0, M + 1 : M + 2, :128].astype(jnp.int32)
-            return (slot, drawn, halo[k, 0, M + 2 : M + 3, :128])
+            drawn = halo[k, M + 1 : M + 2, :128].astype(jnp.int32)
+            return (slot, drawn, halo[k, M + 2 : M + 3, :128])
 
         sides = ((0, has_left, left), (1, has_right, right))
-
-        columns_first()
 
         @pl.when(is_last)
         def _():
             prepare(w, y, pr, wb, yrow, rrow)
 
+        columns_first()
+
+        @pl.when(is_last)
+        def _():
+
             ends = scaled_blocks((0, 1, REG - 1, REG - 2), sc, wb, yrow, rrow)
-            edge[0, 0], edge[0, 1] = with_extras(ends[0], 0), ends[1]
-            edge[1, 0], edge[1, 1] = with_extras(ends[2], REG - 1), ends[3]
+            edge[0] = payload(ends[0], ends[1], 0)
+            edge[1] = payload(ends[2], ends[3], REG - 1)
             pl.semaphore_wait(
                 barrier, 1 + has_left.astype(jnp.int32) + has_right.astype(jnp.int32))
             for k, there, where in sides:
@@ -326,71 +379,71 @@
             for r in (1, 2, 3, 12, 13, 14):
                 gram[r + 1] = region_gram(r, blocks)
 
-            for k, there, where in sides:
-                @pl.when(there)
-                def _(k=k, where=where):
-                    block_copy(1 - k, where).wait_recv()
-                    block_copy(k, where).wait_send()
-
-                @pl.when(jnp.logical_not(there))
-                def _(k=k):
-                    halo[k] = jnp.zeros((2, MX, KB), F32)
-            blocks[-1] = block_terms(halo[0, 0], (0, 1))
-            blocks[-2] = block_terms(halo[0, 1], (0,))
-            blocks[16] = block_terms(halo[1, 0], (1, 2))
-            blocks[17] = block_terms(halo[1, 1], (2,))
-            for r in (-1, 0, 15, 16):
+            await_halo(1)
+            near, far = received(1)
+            blocks[16] = block_terms(near, (1, 2))
+            blocks[17] = block_terms(far, (2,))
+            for r in (15, 16):
                 gram[r + 1] = region_gram(r, blocks)
 
-            items = [item(r) for r in ODD_REGIONS[:8]]
-            items += [outside_item(0, 0), outside_item(1, REG + 1)]
-            maps = transforms_group(items, gram, ys, zs)
-            for k, slab in enumerate(pack(maps[:8]) + [m.astype(BF16) for m in maps[8:]]):
+            items = [outside_item(1, 17) if r == 16 else item(r) for r in ODD_REGIONS]
+            for k, slab in enumerate(pack(transforms_group(items, gram, ys, zs))):
                 t[k] = slab
             gram_copy().wait_send()
-
-        @pl.when(jnp.logical_not(is_last))
-        def _():
-            pl.semaphore_wait(barrier, 1 + (lag < last - 1).astype(jnp.int32))
-
-            @pl.when(lag < last - 1)
-            def _():
-                pl.semaphore_signal(
-                    ready, inc=1, device_id={"lag": lag + 2}, device_id_type=MESH)
+            pl.semaphore_wait(ready, 3)
+            each_side(0, start)
+            each_direct(0, start)
+
+            await_halo(0)
+            near, far = received(0)
+            blocks[-1] = block_terms(near, (0, 1))
+            blocks[-2] = block_terms(far, (0,))
+            for r in LATE_REGIONS:
+                gram[r + 1] = region_gram(r, blocks)
+            items = [outside_item(0, 0), item(0)]
+            for k, m in enumerate(transforms_group(items, gram, ys, zs)):
+                t[5 + k] = m.astype(BF16)
+            for back in (6, 4, 2, 1):
+                late(back).start()
+            each_side(7, arrived)
+            each_direct(0, sent)
+            each_side(0, sent)
+            for back in (6, 4, 2, 1):
+                late(back).wait_send()
 
         @pl.when(lag == last - 1)
         def _():
+            pl.semaphore_wait(barrier, 1)
             gram_copy().wait_recv()
             maps = transforms_group([item(r) for r in EVEN_REGIONS], gram, ys, zs)
             for k, slab in enumerate(pack(maps)):
                 t[7 + k] = slab
-
-        @pl.when(lag >= 2)
+            pl.semaphore_wait(ready, 3)
+            each_side(7, start)
+            each_direct(7, start)
+            each_side(0, arrived)
+            late(1).wait_recv()
+            each_direct(7, sent)
+            each_side(7, sent)
+
+        @pl.when(lag < last - 1)
         def _():
-            pl.semaphore_wait(ready, 1)
-
-        for parity, own, other in ((1, ODD_PIECES, EVEN_PIECES), (0, EVEN_PIECES, ODD_PIECES)):
-            @pl.when(odd == parity)
-            def _(own=own, other=other):
-                for k in range(3):
-                    @pl.when(lag < last - 1)
-                    def _(k=k):
-                        onward(k, own).wait_recv()
-
-                    side(k, own).start()
-
-                    @pl.when(lag >= 2)
-                    def _(k=k):
-                        onward(k, own).start()
-
-                for k in range(3):
-                    side(k, other).wait_recv()
-                for k in range(3):
-                    side(k, own).wait_send()
-
-                    @pl.when(lag >= 2)
-                    def _(k=k):
-                        onward(k, own).wait_send()
+            pl.semaphore_wait(barrier, 2)
+            pl.semaphore_signal(
+                ready, inc=1, device_id={"lag": last - 1 + odd}, device_id_type=MESH)
+            for parity, own, other in ((1, 0, 7), (0, 7, 0)):
+                @pl.when(odd == parity)
+                def _(parity=parity, own=own, other=other):
+                    for k in range(len(PIECES)):
+                        direct(k, own, 2).wait_recv()
+                        side(k, own).start()
+                    each_side(other, arrived)
+                    late(1).wait_recv()
+                    if parity == 1:
+                        late(1).start()
+                    each_side(own, sent)
+                    if parity == 1:
+                        late(1).wait_send()
 
         t_out[...] = t[...]
 
@@ -419,14 +472,15 @@
             pltpu.VMEM((WIDTH * 128, KB), BF16),
             pltpu.VMEM((REG, KB), F32),
             pltpu.VMEM((REG, KB), F32),
-            pltpu.VMEM((2, 2, MX, KB), F32),
-            pltpu.VMEM((2, 2, MX, KB), F32),
+            pltpu.VMEM((2, 88, 384), F32),
+            pltpu.VMEM((2, 88, 384), F32),
             pltpu.VMEM((REG + 2, MX, 128), F32),
             pltpu.VMEM((SLABS, M, 128), BF16),
-            pltpu.VMEM((10, M, 256), BF16),
-            pltpu.VMEM((10, M, 256), BF16),
+            pltpu.VMEM((8, M, 256), BF16),
+            pltpu.VMEM((8, M, 256), BF16),
             dma((5,)), dma((4,)), dma((2,)), dma((2,)), dma, dma,
-            dma((3,)), dma((3,)), dma((3,)), dma((3,)), pltpu.SemaphoreType.REGULAR,
+            dma((2, 3)), dma((2,)), dma((2,)), dma((2,)), dma((4,)), dma,
+            pltpu.SemaphoreType.REGULAR,
         ],
         compiler_params=pltpu.CompilerParams(
             collective_id=0, has_side_effects=True, vmem_limit_bytes=24 * 2**20),
@@ -437,7 +491,7 @@
     base = lax.axis_index("space") * REG - 1
     slabs = [t[k].astype(F32) for k in range(SLABS)]
     maps = unpack(slabs[:5]) + slabs[5:7] + unpack(slabs[7:])
-    for r, m in zip(ODD_REGIONS + EVEN_REGIONS, maps):
+    for r, m in zip(ODD_REGIONS + LATE_REGIONS + EVEN_REGIONS, maps):
         tf[r + 1] = m
 
     def column(c):

time: 40.8 us -> 38 us (0.931)
  Pallas kernels: 40.5 us -> 37.7 us
    pallas_call x1, Pallas kernels: 35.7 us -> 32.9 us  [transforms_call(): pl.pallas_call(make_transform_kernel(lags, spaces), out_shape=(jax.ShapeD...]
where the time goes in v3:
time: 38 us; the launch traced here: 37.9 us
  Pallas kernels  37.7 us (99%)
    pallas_call x1, Pallas kernels, transforms_call(): pl.pallas_call(make_transform_kernel(lags, spaces), out_shape=(jax.ShapeD...  32.9 us
    pallas_call x1, Pallas kernels, analysis_call(): pl.pallas_call(analysis_kernel, out_shape=jax.ShapeDtypeStruct((LEV, M, C...  4.77 us

profile of v3, /device:TPU:7, one launch (start us, length us, event | category | flops | bytes accessed | tf_op | source)
XLA Modules:
  0.0 37.9 jit_solution(3793928843773492849)
XLA Ops:
  0.0 0.0 copy-start.1
  0.0 0.0 copy-start
  0.0 32.9 %shard_map.82 = (bf16[12,80,128]{2,1,0:T(8,128)(2,1)S(1)}, bf16[128,128,128]{2,1,0:T(8,128)(2,1)S(1)}) custom-call(bf16[127,80,128]{2,1,0:T(8,128)(2,1)} %bitcast.6, bf16[24,127]{1,0:T(8,128)(2,1)} %w_hbm.1, f32[24,128]{1,0:T(8,128)} %y_hbm.1, f32[24,128]{1,0:T(8,128)} %pr_hbm.1, s32[16,80]{1,0:T(8,128)} %resample_hbm.1, f32[16]{0:T(128)} %blend_hbm.1), custom_call_target="tpu_custom_call" | custom-call | tf_op jit(solution)/shard_map/pallas_call | solution.py:457
  32.9 0.0 copy-done.1
  32.9 0.0 copy-done
  32.9 4.8 %shard_map.83 = bf16[127,80,128]{2,1,0:T(8,128)(2,1)} custom-call(bf16[128,128,128]{2,1,0:T(8,128)(2,1)S(1)} %get-tuple-element.7.s, bf16[12,80,128]{2,1,0:T(8,128)(2,1)S(1)} %get-tuple-element.8.t, s32[128]{0:T(128)S(1)} %copy-done, f32[128]{0:T(128)S(1)} %copy-done.1), custom_call_target="tpu_custom_call" | custom-call | tf_op jit(solution)/shard_map/pallas_call | solution.py:524
Async XLA Ops:
  0.0 32.9 %copy-start.1 = (f32[128]{0:T(128)S(1)}, f32[128]{0:T(128)}, u32[]{:S(2)}) copy-start(f32[128]{0:T(128)} %weight.1) | copy-start | bytes 1540
  0.0 32.9 %copy-start = (s32[128]{0:T(128)S(1)}, s32[128]{0:T(128)}, u32[]{:S(2)}) copy-start(s32[128]{0:T(128)} %near.1) | copy-start | bytes 1540

commit v4 on v3

--- a/solution.py
+++ b/solution.py
@@ -187,12 +187,18 @@
 LEVEL_CHUNKS = ((0, 32), (32, 32), (64, 32), (96, 31))
 
 
+def analyse(c, base, near, weight, maps, states, out):
+    share = weight[c]
+    mixed = share * maps[c // WIDTH + 1] + (1.0 - share) * maps[jnp.clip(near[c] - base, 0, maps.shape[0] - 1)]
+    out[c] = jnp.dot(states[c, :, :M], mixed.astype(BF16), preferred_element_type=F32).astype(BF16)
+
+
 def make_transform_kernel(lags, spaces):
     last = lags - 1
 
     def kernel(
-        st_hbm, w_hbm, y_hbm, pr_hbm, resample_hbm, blend_hbm, t_out, sc,
-        st, w, y, pr, resample, blend,
+        st_hbm, w_hbm, y_hbm, pr_hbm, resample_hbm, blend_hbm, near_hbm, weight_hbm, t_out, sc,
+        st, w, y, pr, resample, blend, near, weight, tf,
         wb, yrow, rrow, edge, halo, gram, t, ys, zs,
         in_sem, st_sem, x_send, x_recv, g_send, g_recv,
         p_next, p_side, own_recv, other_recv, f_send, f_recv, ready,
@@ -216,6 +222,10 @@
             for back in (6, 4, 2):
                 greet({"lag": lag - back})
 
+        @pl.when((lag == 2) | (lag == 3))
+        def _():
+            greet({"lag": lag + 2})
+
         @pl.when(is_last)
         def _():
             @pl.when(has_left)
@@ -234,7 +244,8 @@
         small = [
             pltpu.make_async_copy(src, dst, in_sem.at[k])
             for k, (src, dst) in enumerate(
-                ((w_hbm, w), (y_hbm, y), (pr_hbm, pr), (resample_hbm, resample), (blend_hbm, blend)))
+                ((w_hbm, w), (y_hbm, y), (pr_hbm, pr), (resample_hbm, resample), (blend_hbm, blend),
+                 (near_hbm, near), (weight_hbm, weight)))
         ]
         for copy in small:
             copy.start()
@@ -272,7 +283,7 @@
                 device_id={"lag": lag - back}, device_id_type=MESH)
 
         def each_direct(first, act):
-            for back in (6, 4, 2):
+            for back in (2, 6):
                 for k in range(len(PIECES)):
                     act(direct(k, first, back))
 
@@ -309,24 +320,12 @@
         def item(r):
             return (r + 1, wide_row(r), blend[r])
 
-        def payload(near, far, r):
+        def with_extras(partial, r):
             values = jnp.concatenate(
-                [drawn_row(r).astype(F32), jnp.zeros((1, KB - M), F32)], axis=1)
-            which = lax.broadcasted_iota(jnp.int32, (88, KB), 0)
-            near = jnp.where(
-                which == M + 1, values, jnp.where(which == M + 2, blend[r], near[:88]))
-            lane = lax.broadcasted_iota(jnp.int32, (88, 128), 1)
-            both = jnp.where(lane < 64, near[:, 128:], pltpu.roll(far[:88, 128:], 64, 1))
-            return jnp.concatenate([near[:, :128], both, far[:88, :128]], axis=1)
-
-        def received(k):
-            lane = lax.broadcasted_iota(jnp.int32, (88, 128), 1)
-            both = halo[k, :, 128:256]
-            near = jnp.concatenate([halo[k, :, :128], jnp.where(lane < 64, both, 0.0)], axis=1)
-            far = jnp.concatenate(
-                [halo[k, :, 256:], jnp.where(lane < 64, pltpu.roll(both, 64, 1), 0.0)], axis=1)
-            gap = jnp.zeros((MX - 88, KB), F32)
-            return (jnp.concatenate([near, gap], axis=0), jnp.concatenate([far, gap], axis=0))
+                [drawn_row(r).astype(F32), jnp.zeros((1, 128 - M), F32)], axis=1)
+            which = lax.broadcasted_iota(jnp.int32, (MX, 128), 0)
+            return jnp.where(
+                which == M + 1, values, jnp.where(which == M + 2, blend[r], partial))
 
         def await_halo(k):
             there, where = ((has_left, left), (has_right, right))[k]
@@ -338,11 +337,11 @@
 
             @pl.when(jnp.logical_not(there))
             def _():
-                halo[k] = jnp.zeros((88, 384), F32)
+                halo[k] = jnp.zeros((2, MX, 128), F32)
 
         def outside_item(k, slot):
-            drawn = halo[k, M + 1 : M + 2, :128].astype(jnp.int32)
-            return (slot, drawn, halo[k, M + 2 : M + 3, :128])
+            drawn = halo[k, 1, M + 1 : M + 2, :].astype(jnp.int32)
+            return (slot, drawn, halo[k, 1, M + 2 : M + 3, :])
 
         sides = ((0, has_left, left), (1, has_right, right))
 
@@ -356,8 +355,13 @@
         def _():
 
             ends = scaled_blocks((0, 1, REG - 1, REG - 2), sc, wb, yrow, rrow)
-            edge[0] = payload(ends[0], ends[1], 0)
-            edge[1] = payload(ends[2], ends[3], REG - 1)
+            blocks = {}
+            for r, x in zip((0, 1, 15, 14), ends):
+                blocks[r] = block_terms(x, (0, 1, 2))
+            edge[0, 0] = gram_of([blocks[0][2]])
+            edge[0, 1] = with_extras(gram_of([blocks[0][1], blocks[1][2]]), 0)
+            edge[1, 0] = gram_of([blocks[15][0]])
+            edge[1, 1] = with_extras(gram_of([blocks[14][0], blocks[15][1]]), REG - 1)
             pl.semaphore_wait(
                 barrier, 1 + has_left.astype(jnp.int32) + has_right.astype(jnp.int32))
             for k, there, where in sides:
@@ -366,7 +370,6 @@
                     block_copy(k, where).start()
 
             inner = tuple(range(3, 13))
-            blocks = {}
             for r, x in zip(inner, scaled_blocks(inner, sc, wb, yrow, rrow)):
                 blocks[r] = block_terms(x, (0, 1, 2))
             for r in EVEN_REGIONS:
@@ -374,17 +377,12 @@
             gram_copy().start()
             for r, x in zip((2, 13), scaled_blocks((2, 13), sc, wb, yrow, rrow)):
                 blocks[r] = block_terms(x, (0, 1, 2))
-            for r, x in zip((0, 1, 15, 14), ends):
-                blocks[r] = block_terms(x, (0, 1, 2))
             for r in (1, 2, 3, 12, 13, 14):
                 gram[r + 1] = region_gram(r, blocks)
 
             await_halo(1)
-            near, far = received(1)
-            blocks[16] = block_terms(near, (1, 2))
-            blocks[17] = block_terms(far, (2,))
-            for r in (15, 16):
-                gram[r + 1] = region_gram(r, blocks)
+            gram[REG] = edge[1, 1] + halo[1, 0]
+            gram[REG + 1] = edge[1, 0] + halo[1, 1]
 
             items = [outside_item(1, 17) if r == 16 else item(r) for r in ODD_REGIONS]
             for k, slab in enumerate(pack(transforms_group(items, gram, ys, zs))):
@@ -395,21 +393,14 @@
             each_direct(0, start)
 
             await_halo(0)
-            near, far = received(0)
-            blocks[-1] = block_terms(near, (0, 1))
-            blocks[-2] = block_terms(far, (0,))
-            for r in LATE_REGIONS:
-                gram[r + 1] = region_gram(r, blocks)
+            gram[1] = edge[0, 1] + halo[0, 0]
+            gram[0] = edge[0, 0] + halo[0, 1]
             items = [outside_item(0, 0), item(0)]
             for k, m in enumerate(transforms_group(items, gram, ys, zs)):
                 t[5 + k] = m.astype(BF16)
             for back in (6, 4, 2, 1):
                 late(back).start()
             each_side(7, arrived)
-            each_direct(0, sent)
-            each_side(0, sent)
-            for back in (6, 4, 2, 1):
-                late(back).wait_send()
 
         @pl.when(lag == last - 1)
         def _():
@@ -422,13 +413,10 @@
             each_side(7, start)
             each_direct(7, start)
             each_side(0, arrived)
-            late(1).wait_recv()
-            each_direct(7, sent)
-            each_side(7, sent)
 
         @pl.when(lag < last - 1)
         def _():
-            pl.semaphore_wait(barrier, 2)
+            pl.semaphore_wait(barrier, 2 + (lag >= 4).astype(jnp.int32))
             pl.semaphore_signal(
                 ready, inc=1, device_id={"lag": last - 1 + odd}, device_id_type=MESH)
             for parity, own, other in ((1, 0, 7), (0, 7, 0)):
@@ -436,31 +424,73 @@
                 def _(parity=parity, own=own, other=other):
                     for k in range(len(PIECES)):
                         direct(k, own, 2).wait_recv()
+
+                        @pl.when(lag >= 4)
+                        def _(k=k):
+                            direct(k, own, 2).start()
+
                         side(k, own).start()
                     each_side(other, arrived)
+
+        for regions, first in ((ODD_REGIONS, 0), (EVEN_REGIONS, 7)):
+            for r, m in zip(regions, unpack([t[first + k].astype(F32) for k in range(5)])):
+                tf[r + 1] = m
+
+        @pl.loop(1, COLS // 16)
+        def _(group):
+            for i in range(16):
+                analyse(group * 16 + i, here * REG - 1, near, weight, tf, sc, sc)
+
+        @pl.when(is_last)
+        def _():
+            each_direct(0, sent)
+            each_side(0, sent)
+            for back in (6, 4, 2, 1):
+                late(back).wait_send()
+
+        @pl.when(lag == last - 1)
+        def _():
+            late(1).wait_recv()
+            each_direct(7, sent)
+            each_side(7, sent)
+
+        @pl.when(lag < last - 1)
+        def _():
+            for parity, own in ((1, 0), (0, 7)):
+                @pl.when(odd == parity)
+                def _(parity=parity, own=own):
                     late(1).wait_recv()
                     if parity == 1:
                         late(1).start()
                     each_side(own, sent)
+
+                    @pl.when(lag >= 4)
+                    def _():
+                        for k in range(len(PIECES)):
+                            direct(k, own, 2).wait_send()
+
                     if parity == 1:
                         late(1).wait_send()
 
-        t_out[...] = t[...]
+        t_out[0] = t[5].astype(F32)
+        t_out[1] = t[6].astype(F32)
+        t_out[2] = tf[2]
+        t_out[3] = tf[3]
 
     return kernel
 
 
-def transforms_call(lags, spaces, st, w, y, pr, resample, blend):
+def transforms_call(lags, spaces, *operands):
     vmem = pl.BlockSpec(memory_space=pltpu.VMEM)
     hbm = pl.BlockSpec(memory_space=pltpu.HBM)
     dma = pltpu.SemaphoreType.DMA
     return pl.pallas_call(
         make_transform_kernel(lags, spaces),
         out_shape=(
-            jax.ShapeDtypeStruct((SLABS, M, 128), BF16),
+            jax.ShapeDtypeStruct((4, M, 128), F32),
             jax.ShapeDtypeStruct((COLS, 128, 128), BF16),
         ),
-        in_specs=[hbm] * 6,
+        in_specs=[hbm] * 8,
         out_specs=(vmem, vmem),
         scratch_shapes=[
             pltpu.VMEM((LEV, M, COLS), BF16),
@@ -469,38 +499,31 @@
             pltpu.VMEM((NOBS, COLS), F32),
             pltpu.VMEM((REG, M), jnp.int32),
             pltpu.SMEM((REG,), F32),
+            pltpu.SMEM((COLS,), jnp.int32),
+            pltpu.SMEM((COLS,), F32),
+            pltpu.VMEM((REG + 2, M, 128), F32),
             pltpu.VMEM((WIDTH * 128, KB), BF16),
             pltpu.VMEM((REG, KB), F32),
             pltpu.VMEM((REG, KB), F32),
-            pltpu.VMEM((2, 88, 384), F32),
-            pltpu.VMEM((2, 88, 384), F32),
+            pltpu.VMEM((2, 2, MX, 128), F32),
+            pltpu.VMEM((2, 2, MX, 128), F32),
             pltpu.VMEM((REG + 2, MX, 128), F32),
             pltpu.VMEM((SLABS, M, 128), BF16),
             pltpu.VMEM((8, M, 256), BF16),
             pltpu.VMEM((8, M, 256), BF16),
-            dma((5,)), dma((4,)), dma((2,)), dma((2,)), dma, dma,
+            dma((7,)), dma((4,)), dma((2,)), dma((2,)), dma, dma,
             dma((2, 3)), dma((2,)), dma((2,)), dma((2,)), dma((4,)), dma,
             pltpu.SemaphoreType.REGULAR,
         ],
         compiler_params=pltpu.CompilerParams(
             collective_id=0, has_side_effects=True, vmem_limit_bytes=24 * 2**20),
-    )(*(pltpu.with_memory_space_constraint(x, pltpu.HBM) for x in (st, w, y, pr, resample, blend)))
-
-
-def analysis_kernel(s, t, near, weight, out, tf, o, ov, o_sem):
+    )(*(pltpu.with_memory_space_constraint(x, pltpu.HBM) for x in operands))
+
+
+def analysis_kernel(s, t, near, weight, out, o, ov, o_sem):
     base = lax.axis_index("space") * REG - 1
-    slabs = [t[k].astype(F32) for k in range(SLABS)]
-    maps = unpack(slabs[:5]) + slabs[5:7] + unpack(slabs[7:])
-    for r, m in zip(ODD_REGIONS + LATE_REGIONS + EVEN_REGIONS, maps):
-        tf[r + 1] = m
-
-    def column(c):
-        share = weight[c]
-        maps = (share * tf[c // WIDTH + 1] + (1.0 - share) * tf[near[c] - base]).astype(BF16)
-        o[c] = jnp.dot(s[c, :, :M], maps, preferred_element_type=F32).astype(BF16)
-
-    for c in range(COLS):
-        column(c)
+    for c in range(2 * WIDTH):
+        analyse(c, base, near, weight, t, s, o)
 
     def store(k):
         first = k * 16
@@ -510,7 +533,8 @@
 
     for k in range(8):
         first, stop = k * 16, min(k * 16 + 16, LEV)
-        turned = jnp.transpose(o[:, first : first + 16, :M], (1, 2, 0))
+        part = [ref[:, first : first + 16, :M] for ref in (o, s.at[pl.ds(16, COLS - 16)])]
+        turned = jnp.transpose(jnp.concatenate(part, axis=0), (1, 2, 0))
         ov[first:stop] = turned[: stop - first]
         store(k).start()
     for k in range(8):
@@ -527,8 +551,7 @@
         in_specs=[vmem, vmem, smem, smem],
         out_specs=hbm,
         scratch_shapes=[
-            pltpu.VMEM((REG + 2, M, 128), F32),
-            pltpu.VMEM((COLS, 128, 128), BF16),
+            pltpu.VMEM((2 * WIDTH, 128, 128), BF16),
             pltpu.VMEM((LEV, M, COLS), BF16),
             pltpu.SemaphoreType.DMA((8,)),
         ],
@@ -543,7 +566,8 @@
     st = jnp.transpose(states[0], (1, 0, 2))
     t, s = transforms_call(
         lax.axis_size("lag"), lax.axis_size("space"),
-        st, obs_weights, observations, obs_precision, resample_index, blend_weight)
+        st, obs_weights, observations, obs_precision, resample_index, blend_weight,
+        stencil_region, stencil_weight)
     out = analysis_call(s, t, stencil_region, stencil_weight)
     return jnp.transpose(out, (1, 0, 2))[None]
 

time: 38 us -> 39.4 us (1.037)
  the two profiles are of different devices: /device:TPU:7 before, /device:TPU:15 now
where the time goes in v4:
time: 39.4 us; the launch traced here: 39.3 us
  Pallas kernels  39.1 us (99%)
    pallas_call x1, Pallas kernels, transforms_call(): pl.pallas_call(make_transform_kernel(lags, spaces), out_shape=(jax.ShapeD...  35.4 us
    pallas_call x1, Pallas kernels, analysis_call(): pl.pallas_call(analysis_kernel, out_shape=jax.ShapeDtypeStruct((LEV, M, C...  3.64 us

profile of v4, /device:TPU:15, one launch (start us, length us, event | category | flops | bytes accessed | tf_op | source)
XLA Modules:
  0.0 39.3 jit_solution(15181470011959212664)
XLA Ops:
  0.0 0.0 copy-start.1
  0.0 0.0 copy-start
  0.0 35.4 %shard_map.82 = (f32[4,80,128]{2,1,0:T(8,128)S(1)}, bf16[128,128,128]{2,1,0:T(8,128)(2,1)S(1)}) custom-call(bf16[127,80,128]{2,1,0:T(8,128)(2,1)} %bitcast.6, bf16[24,127]{1,0:T(8,128)(2,1)} %w_hbm.1, f32[24,128]{1,0:T(8,128)} %y_hbm.1, f32[24,128]{1,0:T(8,128)} %pr_hbm.1, s32[16,80]{1,0:T(8,128)} %resample_hbm.1, f32[16]{0:T(128)} %blend_hbm.1, s32[128]{0:T(128)} %near.1, ...), custom_call_target="tpu_custom_call" | custom-call | tf_op jit(solution)/shard_map/pallas_call | solution.py:487
  35.4 0.0 copy-done.1
  35.4 0.0 copy-done
  35.5 3.6 %shard_map.83 = bf16[127,80,128]{2,1,0:T(8,128)(2,1)} custom-call(bf16[128,128,128]{2,1,0:T(8,128)(2,1)S(1)} %get-tuple-element.7.s, f32[4,80,128]{2,1,0:T(8,128)S(1)} %get-tuple-element.8.t, s32[128]{0:T(128)S(1)} %copy-done, f32[128]{0:T(128)S(1)} %copy-done.1), custom_call_target="tpu_custom_call" | custom-call | tf_op jit(solution)/shard_map/pallas_call | solution.py:548
Async XLA Ops:
  0.0 35.4 %copy-start.1 = (f32[128]{0:T(128)S(1)}, f32[128]{0:T(128)}, u32[]{:S(2)}) copy-start(f32[128]{0:T(128)} %weight.1) | copy-start | bytes 1540
  0.0 35.4 %copy-start = (s32[128]{0:T(128)S(1)}, s32[128]{0:T(128)}, u32[]{:S(2)}) copy-start(s32[128]{0:T(128)} %near.1) | copy-start | bytes 1540

commit v5 on v3

--- a/solution.py
+++ b/solution.py
@@ -309,24 +309,12 @@
         def item(r):
             return (r + 1, wide_row(r), blend[r])
 
-        def payload(near, far, r):
+        def with_extras(partial, r):
             values = jnp.concatenate(
-                [drawn_row(r).astype(F32), jnp.zeros((1, KB - M), F32)], axis=1)
-            which = lax.broadcasted_iota(jnp.int32, (88, KB), 0)
-            near = jnp.where(
-                which == M + 1, values, jnp.where(which == M + 2, blend[r], near[:88]))
-            lane = lax.broadcasted_iota(jnp.int32, (88, 128), 1)
-            both = jnp.where(lane < 64, near[:, 128:], pltpu.roll(far[:88, 128:], 64, 1))
-            return jnp.concatenate([near[:, :128], both, far[:88, :128]], axis=1)
-
-        def received(k):
-            lane = lax.broadcasted_iota(jnp.int32, (88, 128), 1)
-            both = halo[k, :, 128:256]
-            near = jnp.concatenate([halo[k, :, :128], jnp.where(lane < 64, both, 0.0)], axis=1)
-            far = jnp.concatenate(
-                [halo[k, :, 256:], jnp.where(lane < 64, pltpu.roll(both, 64, 1), 0.0)], axis=1)
-            gap = jnp.zeros((MX - 88, KB), F32)
-            return (jnp.concatenate([near, gap], axis=0), jnp.concatenate([far, gap], axis=0))
+                [drawn_row(r).astype(F32), jnp.zeros((1, 128 - M), F32)], axis=1)
+            which = lax.broadcasted_iota(jnp.int32, (MX, 128), 0)
+            return jnp.where(
+                which == M + 1, values, jnp.where(which == M + 2, blend[r], partial))
 
         def await_halo(k):
             there, where = ((has_left, left), (has_right, right))[k]
@@ -338,11 +326,11 @@
 
             @pl.when(jnp.logical_not(there))
             def _():
-                halo[k] = jnp.zeros((88, 384), F32)
+                halo[k] = jnp.zeros((2, MX, 128), F32)
 
         def outside_item(k, slot):
-            drawn = halo[k, M + 1 : M + 2, :128].astype(jnp.int32)
-            return (slot, drawn, halo[k, M + 2 : M + 3, :128])
+            drawn = halo[k, 1, M + 1 : M + 2, :].astype(jnp.int32)
+            return (slot, drawn, halo[k, 1, M + 2 : M + 3, :])
 
         sides = ((0, has_left, left), (1, has_right, right))
 
@@ -356,8 +344,13 @@
         def _():
 
             ends = scaled_blocks((0, 1, REG - 1, REG - 2), sc, wb, yrow, rrow)
-            edge[0] = payload(ends[0], ends[1], 0)
-            edge[1] = payload(ends[2], ends[3], REG - 1)
+            blocks = {}
+            for r, x in zip((0, 1, 15, 14), ends):
+                blocks[r] = block_terms(x, (0, 1, 2))
+            edge[0, 0] = gram_of([blocks[0][2]])
+            edge[0, 1] = with_extras(gram_of([blocks[0][1], blocks[1][2]]), 0)
+            edge[1, 0] = gram_of([blocks[15][0]])
+            edge[1, 1] = with_extras(gram_of([blocks[14][0], blocks[15][1]]), REG - 1)
             pl.semaphore_wait(
                 barrier, 1 + has_left.astype(jnp.int32) + has_right.astype(jnp.int32))
             for k, there, where in sides:
@@ -366,7 +359,6 @@
                     block_copy(k, where).start()
 
             inner = tuple(range(3, 13))
-            blocks = {}
             for r, x in zip(inner, scaled_blocks(inner, sc, wb, yrow, rrow)):
                 blocks[r] = block_terms(x, (0, 1, 2))
             for r in EVEN_REGIONS:
@@ -374,17 +366,12 @@
             gram_copy().start()
             for r, x in zip((2, 13), scaled_blocks((2, 13), sc, wb, yrow, rrow)):
                 blocks[r] = block_terms(x, (0, 1, 2))
-            for r, x in zip((0, 1, 15, 14), ends):
-                blocks[r] = block_terms(x, (0, 1, 2))
             for r in (1, 2, 3, 12, 13, 14):
                 gram[r + 1] = region_gram(r, blocks)
 
             await_halo(1)
-            near, far = received(1)
-            blocks[16] = block_terms(near, (1, 2))
-            blocks[17] = block_terms(far, (2,))
-            for r in (15, 16):
-                gram[r + 1] = region_gram(r, blocks)
+            gram[REG] = edge[1, 1] + halo[1, 0]
+            gram[REG + 1] = edge[1, 0] + halo[1, 1]
 
             items = [outside_item(1, 17) if r == 16 else item(r) for r in ODD_REGIONS]
             for k, slab in enumerate(pack(transforms_group(items, gram, ys, zs))):
@@ -395,11 +382,8 @@
             each_direct(0, start)
 
             await_halo(0)
-            near, far = received(0)
-            blocks[-1] = block_terms(near, (0, 1))
-            blocks[-2] = block_terms(far, (0,))
-            for r in LATE_REGIONS:
-                gram[r + 1] = region_gram(r, blocks)
+            gram[1] = edge[0, 1] + halo[0, 0]
+            gram[0] = edge[0, 0] + halo[0, 1]
             items = [outside_item(0, 0), item(0)]
             for k, m in enumerate(transforms_group(items, gram, ys, zs)):
                 t[5 + k] = m.astype(BF16)
@@ -472,8 +456,8 @@
             pltpu.VMEM((WIDTH * 128, KB), BF16),
             pltpu.VMEM((REG, KB), F32),
             pltpu.VMEM((REG, KB), F32),
-            pltpu.VMEM((2, 88, 384), F32),
-            pltpu.VMEM((2, 88, 384), F32),
+            pltpu.VMEM((2, 2, MX, 128), F32),
+            pltpu.VMEM((2, 2, MX, 128), F32),
             pltpu.VMEM((REG + 2, MX, 128), F32),
             pltpu.VMEM((SLABS, M, 128), BF16),
             pltpu.VMEM((8, M, 256), BF16),

time: 38 us -> 37.5 us (0.987)
  Pallas kernels: 37.7 us -> 37.2 us
    pallas_call x1, Pallas kernels: 32.9 us -> 32.4 us  [transforms_call(): pl.pallas_call(make_transform_kernel(lags, spaces), out_shape=(jax.ShapeD...]
where the time goes in v5:
time: 37.5 us; the launch traced here: 37.4 us
  Pallas kernels  37.2 us (99%)
    pallas_call x1, Pallas kernels, transforms_call(): pl.pallas_call(make_transform_kernel(lags, spaces), out_shape=(jax.ShapeD...  32.4 us
    pallas_call x1, Pallas kernels, analysis_call(): pl.pallas_call(analysis_kernel, out_shape=jax.ShapeDtypeStruct((LEV, M, C...  4.77 us

profile of v5, /device:TPU:7, one launch (start us, length us, event | category | flops | bytes accessed | tf_op | source)
XLA Modules:
  0.0 37.4 jit_solution(12556419858842514291)
XLA Ops:
  0.0 0.0 copy-start.1
  0.0 0.0 copy-start
  0.0 32.4 %shard_map.82 = (bf16[12,80,128]{2,1,0:T(8,128)(2,1)S(1)}, bf16[128,128,128]{2,1,0:T(8,128)(2,1)S(1)}) custom-call(bf16[127,80,128]{2,1,0:T(8,128)(2,1)} %bitcast.6, bf16[24,127]{1,0:T(8,128)(2,1)} %w_hbm.1, f32[24,128]{1,0:T(8,128)} %y_hbm.1, f32[24,128]{1,0:T(8,128)} %pr_hbm.1, s32[16,80]{1,0:T(8,128)} %resample_hbm.1, f32[16]{0:T(128)} %blend_hbm.1), custom_call_target="tpu_custom_call" | custom-call | tf_op jit(solution)/shard_map/pallas_call | solution.py:441
  32.4 0.0 copy-done.1
  32.4 0.0 copy-done
  32.4 4.8 %shard_map.83 = bf16[127,80,128]{2,1,0:T(8,128)(2,1)} custom-call(bf16[128,128,128]{2,1,0:T(8,128)(2,1)S(1)} %get-tuple-element.7.s, bf16[12,80,128]{2,1,0:T(8,128)(2,1)S(1)} %get-tuple-element.8.t, s32[128]{0:T(128)S(1)} %copy-done, f32[128]{0:T(128)S(1)} %copy-done.1), custom_call_target="tpu_custom_call" | custom-call | tf_op jit(solution)/shard_map/pallas_call | solution.py:508
Async XLA Ops:
  0.0 32.4 %copy-start.1 = (f32[128]{0:T(128)S(1)}, f32[128]{0:T(128)}, u32[]{:S(2)}) copy-start(f32[128]{0:T(128)} %weight.1) | copy-start | bytes 1540
  0.0 32.4 %copy-start = (s32[128]{0:T(128)S(1)}, s32[128]{0:T(128)}, u32[]{:S(2)}) copy-start(s32[128]{0:T(128)} %near.1) | copy-start | bytes 1540

commit v6 on v5

--- a/solution.py
+++ b/solution.py
@@ -353,7 +353,7 @@
             edge[1, 1] = with_extras(gram_of([blocks[14][0], blocks[15][1]]), REG - 1)
             pl.semaphore_wait(
                 barrier, 1 + has_left.astype(jnp.int32) + has_right.astype(jnp.int32))
-            for k, there, where in sides:
+            for k, there, where in sides[::-1]:
                 @pl.when(there)
                 def _(k=k, where=where):
                     block_copy(k, where).start()

time: 37.5 us -> 37.5 us (level)
  no operation moved by 1% of the time
where the time goes in v6:
time: 37.5 us; the launch traced here: 37.4 us
  Pallas kernels  37.2 us (99%)
    pallas_call x1, Pallas kernels, transforms_call(): pl.pallas_call(make_transform_kernel(lags, spaces), out_shape=(jax.ShapeD...  32.4 us
    pallas_call x1, Pallas kernels, analysis_call(): pl.pallas_call(analysis_kernel, out_shape=jax.ShapeDtypeStruct((LEV, M, C...  4.77 us

profile of v6, /device:TPU:7, one launch (start us, length us, event | category | flops | bytes accessed | tf_op | source)
XLA Modules:
  0.0 37.4 jit_solution(2467405599812925905)
XLA Ops:
  0.0 0.0 copy-start.1
  0.0 0.0 copy-start
  0.0 32.4 %shard_map.82 = (bf16[12,80,128]{2,1,0:T(8,128)(2,1)S(1)}, bf16[128,128,128]{2,1,0:T(8,128)(2,1)S(1)}) custom-call(bf16[127,80,128]{2,1,0:T(8,128)(2,1)} %bitcast.6, bf16[24,127]{1,0:T(8,128)(2,1)} %w_hbm.1, f32[24,128]{1,0:T(8,128)} %y_hbm.1, f32[24,128]{1,0:T(8,128)} %pr_hbm.1, s32[16,80]{1,0:T(8,128)} %resample_hbm.1, f32[16]{0:T(128)} %blend_hbm.1), custom_call_target="tpu_custom_call" | custom-call | tf_op jit(solution)/shard_map/pallas_call | solution.py:441
  32.4 0.0 copy-done.1
  32.4 0.0 copy-done
  32.4 4.8 %shard_map.83 = bf16[127,80,128]{2,1,0:T(8,128)(2,1)} custom-call(bf16[128,128,128]{2,1,0:T(8,128)(2,1)S(1)} %get-tuple-element.7.s, bf16[12,80,128]{2,1,0:T(8,128)(2,1)S(1)} %get-tuple-element.8.t, s32[128]{0:T(128)S(1)} %copy-done, f32[128]{0:T(128)S(1)} %copy-done.1), custom_call_target="tpu_custom_call" | custom-call | tf_op jit(solution)/shard_map/pallas_call | solution.py:508
Async XLA Ops:
  0.0 32.4 %copy-start.1 = (f32[128]{0:T(128)S(1)}, f32[128]{0:T(128)}, u32[]{:S(2)}) copy-start(f32[128]{0:T(128)} %weight.1) | copy-start | bytes 1540
  0.0 32.4 %copy-start = (s32[128]{0:T(128)S(1)}, s32[128]{0:T(128)}, u32[]{:S(2)}) copy-start(s32[128]{0:T(128)} %near.1) | copy-start | bytes 1540
